TPU v7x, 256 devices: a whole 4x4x8 slice. The times are simulated.
256 devices in a mesh: tm: 16 (over x_hi, z), space: 16 (over x_lo, y, core).
Axes of the slice: x: 4 (x_hi: 2, x_lo: 2; x = x_hi * 2 + x_lo), y: 4, z: 8, core: 2. Of those that a mesh axis runs over, the one named last changes fastest.
Arguments:
- forcing: float32 [1024, 128, 2048], P('space', 'tm'), may hold values from -6 to 6
- kappa: float32 [1024, 2048], P('space'), may hold values from 0.12 to 0.24
- diag_coef: float32 [128], P('tm'), may hold values from 0.5 to 1.5
- lower_coef: float32 [128], P('tm'), may hold values from -0.6 to 0.6
- upper_coef: float32 [128], P('tm'), may hold values from -0.6 to 0.6
Outputs:
- result: float32 [1024, 128, 2048], P('space', 'tm')
All inputs are finite; a program needn't handle non-finite values.
Results may differ from a plain program's by a relative error of at most 0.0003.
Values sent between devices are 32-bit elements; how exact they have to be, the bound alone decides.
No kernel may reach another device: no remote copies, remote signals or barrier semaphores. Data moves between devices by JAX's collectives and lax.ppermute only.
A program may use at most 128 MiB of HBM per device.

v0:
```python
import jax
import jax.numpy as jnp
from jax import lax
from jax.sharding import PartitionSpec as P

STEPS = 6


def passed_along(value, axis, steps):
    count = lax.axis_size(axis)
    initial, last = (max(0, -steps), min(count, count - steps))
    return lax.ppermute(value, axis, [(source, source + steps) for source in range(initial, last)])


def padded(array, sides, width):
    for axis, dim in sides:
        size, length = (lax.axis_size(axis), array.shape[dim])
        up = [(i, (i + 1) % size) for i in range(size - 1)]
        down = [(j, i) for i, j in up]
        last = lax.slice_in_dim(array, length - width, length, axis=dim)
        initial = lax.slice_in_dim(array, 0, width, axis=dim)
        before = lax.ppermute(last, axis, up)
        after = lax.ppermute(initial, axis, down)
        array = jnp.concatenate([before, array, after], axis=dim)
    return array


def single_diffusion_step(value_extended, kappa_extended):
    interface_rows = 0.5 * (kappa_extended[1:] + kappa_extended[:-1])
    flux_row_values = interface_rows[:, None, :] * (value_extended[1:] - value_extended[:-1])
    div_rows = flux_row_values[1:] - flux_row_values[:-1]
    interior_slice = value_extended[1:-1]
    kin = kappa_extended[1:-1]
    width = kin.shape[-1]
    column = jnp.arange(width, dtype=jnp.int32)
    last_col = column == width - 1
    first_col = column == 0
    k_east = jnp.where(last_col[None, :], 0.0, jnp.roll(kin, -1, axis=-1))
    k_west = jnp.where(first_col[None, :], 0.0, jnp.roll(kin, 1, axis=-1))
    value_eastward = jnp.where(last_col[None, None, :], 0.0, jnp.roll(interior_slice, -1, axis=-1))
    v_west = jnp.where(first_col[None, None, :], 0.0, jnp.roll(interior_slice, 1, axis=-1))
    east_face = (0.5 * (kin + k_east))[:, None, :]
    west_face = (0.5 * (k_west + kin))[:, None, :]
    div_cols = east_face * (value_eastward - interior_slice) - west_face * (interior_slice - v_west)
    return interior_slice + div_rows + div_cols


def time_mix(fields, diag_coef, lower_coef, upper_coef):
    count = fields.shape[1]
    sent_down = lower_coef[0] * fields[:, 0]
    sent_up = upper_coef[-1] * fields[:, -1]
    from_later = passed_along(sent_down, "tm", -1)
    from_earlier = passed_along(sent_up, "tm", 1)
    slot = jnp.arange(count, dtype=jnp.int32)
    later_local = jnp.roll(lower_coef[None, :, None] * fields, -1, axis=1)
    earlier_local = jnp.roll(upper_coef[None, :, None] * fields, 1, axis=1)
    later_terms = jnp.where((slot == count - 1)[None, :, None], from_later[:, None, :], later_local)
    earlier_terms = jnp.where((slot == 0)[None, :, None], from_earlier[:, None, :], earlier_local)
    return diag_coef[None, :, None] * fields + later_terms + earlier_terms


def diffuse_all(fields, kappa_wide):
    kappa_extended = kappa_wide[STEPS - 1 : kappa_wide.shape[0] - STEPS + 1]

    def advance(step, current):
        wide = padded(current, (("space", 0),), 1)
        return single_diffusion_step(wide, kappa_extended)

    return lax.fori_loop(0, STEPS, advance, fields)


def local(forcing, kappa, diag_coef, lower_coef, upper_coef):
    kappa_wide = padded(kappa, (("space", 0),), STEPS)
    mixed = time_mix(forcing, diag_coef, lower_coef, upper_coef)
    return diffuse_all(mixed, kappa_wide)


def solution(mesh):
    return jax.shard_map(
        local,
        mesh=mesh,
        in_specs=(P("space", "tm", None), P("space", None), P("tm"), P("tm"), P("tm")),
        out_specs=P("space", "tm", None),
        check_vma=False,
    )
```

profile of v0, /device:TPU:29, one launch (start us, length us, event | category | flops | bytes accessed | tf_op | source)
XLA Modules:
  0.0 236.0 jit_solution(16159128980116789360)
XLA Ops:
  1.1 2.7 %collective-permute-start.4 = (f32[6,2048]{1,0:T(8,128)S(1)}, f32[6,2048]{1,0:T(8,128)S(1)}, u32[]{:S(2)}, u32[]{:S(2)}) collective-permute-start(f32[6,2048]{1,0:T(8,128)S(1)} %get-tuple-element.76), channel_id=1, source_target_pairs={{1,0},{2,1},{3,2},{4,3},{5,4},{6,5},{7,6},{8,7},{9,8},{10,9},{11,1... | collective-permute-start | bytes 147464 | tf_op jit(solution)/shard_map/ppermute | solution.py:23
  3.8 5.1 %collective-permute-start.5 = (f32[6,2048]{1,0:T(8,128)S(1)}, f32[6,2048]{1,0:T(8,128)S(1)}, u32[]{:S(2)}, u32[]{:S(2)}) collective-permute-start(f32[6,2048]{1,0:T(8,128)S(1)} %get-tuple-element.77), channel_id=1, source_target_pairs={{0,1},{1,2},{2,3},{3,4},{4,5},{5,6},{6,7},{7,8},{8,9},{9,10},{10,1... | collective-permute-start | bytes 147464 | tf_op jit(solution)/shard_map/ppermute | solution.py:22
  10.2 4.5 %fusion.16 = (f32[64,1,2048]{2,1,0:T(1,128)S(1)}, f32[64,1,2048]{2,1,0:T(1,128)S(1)}) fusion(f32[64,8,2048]{2,1,0:T(8,128)} %param.7), kind=kLoop, calls=%fused_computation.39 | loop fusion | bytes 2097152 | tf_op jit(solution)/shard_map/slice | solution.py:50
  14.7 1.6 fusion.11
  16.3 3.5 %collective-permute-start.3 = (f32[64,2048]{1,0:T(8,128)}, f32[64,2048]{1,0:T(8,128)S(1)}, u32[]{:S(2)}, u32[]{:S(2)}) collective-permute-start(f32[64,2048]{1,0:T(8,128)} %fusion.11), channel_id=1, source_target_pairs={{0,16},{16,32},{32,48},{48,64},{64,80},{80,96},{96,112},{112,128},... | collective-permute-start | bytes 1572872 | tf_op jit(solution)/shard_map/ppermute | solution.py:12
  19.9 1.6 fusion.12
  21.5 5.8 %collective-permute-start.2 = (f32[64,2048]{1,0:T(8,128)}, f32[64,2048]{1,0:T(8,128)}, u32[]{:S(2)}, u32[]{:S(2)}) collective-permute-start(f32[64,2048]{1,0:T(8,128)} %fusion.12), channel_id=1, source_target_pairs={{16,0},{32,16},{48,32},{64,48},{80,64},{96,80},{112,96},{128,112},... | collective-permute-start | bytes 1572872 | tf_op jit(solution)/shard_map/ppermute | solution.py:12
  27.6 2.8 %broadcast_multiply_fusion.1 = (f32[64,8,2048]{2,1,0:T(8,128)}, f32[64,8,2048]{2,1,0:T(8,128)S(1)}) fusion(f32[64,8,2048]{2,1,0:T(8,128)S(1)} %copy-done.3, f32[8]{0:T(128)S(1)} %copy-done.7, f32[8]{0:T(128)S(1)} %copy-done.6), kind=kLoop, calls=%fused_computation.21 | loop fusion | flops 2097152 | bytes 12582976 | tf_op jit(solution)/shard_map/mul | solution.py:56
  31.8 2.5 %slice.150 = f32[64,7,2048]{2,1,0:T(8,128)} slice(f32[64,8,2048]{2,1,0:T(8,128)S(1)} %get-tuple-element.71), slice={[0:64], [1:8], [0:2048]} | slice | bytes 7340032 | tf_op jit(solution)/shard_map/jit(_roll_static)/slice | solution.py:55
  34.2 2.7 %slice.152 = f32[64,1,2048]{2,1,0:T(1,128)S(1)} slice(f32[64,8,2048]{2,1,0:T(8,128)} %get-tuple-element.70), slice={[0:64], [7:8], [0:2048]} | slice | bytes 1048576 | tf_op jit(solution)/shard_map/jit(_roll_static)/slice | solution.py:56
  38.0 7.2 %fusion.9 = f32[64,8,2048]{2,1,0:T(8,128)} fusion(f32[64,1,2048]{2,1,0:T(1,128)S(1)} %slice.151, f32[64,7,2048]{2,1,0:T(8,128)} %slice.150, f32[64,7,2048]{2,1,0:T(8,128)} %bitcast.8, f32[64,1,2048]{2,1,0:T(1,128)S(1)} %slice.152, f32[64,8,2048]{2,1,0:T(8,128)} %param.7, f32[64,2048]{1,0:T(8,128)S(1)} %collective-permute-done.3, ...), kind=kLoop, calls=%fused_computation.19 | loop fusion | flops 7340032 | bytes 17825840 | tf_op jit(solution)/shard_map/add | solution.py:59
  45.3 190.7 %while.11 = (s32[]{:T(128)}, f32[64,8,2048]{2,1,0:T(8,128)}, f32[65,2048]{1,0:T(8,128)S(1)}, f32[66,2048]{1,0:T(8,128)}, f32[64,2048]{1,0:T(8,128)S(1)}, /*index=5*/f32[64,2048]{1,0:T(8,128)}, s32[]{:T(128)}) while((s32[]{:T(128)}, f32[64,8,2048]{2,1,0:T(8,128)}, f32[65,2048]{1,0:T(8,128)S(1)}, f32[66,2048]{1,0:T(8,128)}, ...), condition=%wide.region_1.2_spmd, body=%wide.region_0.1_spmd.sunk | while | flops 17766400 | bytes 109080840 | solution.py:69
  46.1 1.9 collective-permute-start
  48.1 5.8 %collective-permute-start.1 = (f32[1,8,2048]{2,1,0:T(8,128)S(1)}, f32[1,8,2048]{2,1,0:T(8,128)S(1)}, u32[]{:S(2)}, u32[]{:S(2)}) collective-permute-start(f32[1,8,2048]{2,1,0:T(8,128)S(1)} %get-tuple-element.130), channel_id=1, source_target_pairs={{0,1},{1,2},{2,3},{3,4},{4,5},{5,6},{6,7},{7,8},{8,9},{9,10},{10,1... | collective-permute-start | bytes 196616 | tf_op jit(solution)/shard_map/while/body/eval_jaxpr/ppermute | solution.py:22
  53.8 8.1 %fusion.28 = (f32[64,8,2047]{2,1,0:T(8,128)}, f32[64,8,2047]{2,1,0:T(8,128)}) fusion(f32[64,8,2048]{2,1,0:T(8,128)} %get-tuple-element.147), kind=kLoop, calls=%fused_computation.37.clone.1 | loop fusion | bytes 16769024 | tf_op jit(solution)/shard_map/while/body/eval_jaxpr/jit(_roll_static)/slice | solution.py:41
  64.4 4.2 %fusion.26 = f32[65,8,2048]{2,1,0:T(8,128)S(1)} fusion(f32[1,8,2048]{2,1,0:T(8,128)S(1)} %collective-permute-done, f32[64,8,2048]{2,1,0:T(8,128)} %get-tuple-element.147, f32[1,8,2048]{2,1,0:T(8,128)S(1)} %collective-permute-done.1, f32[65,2048]{1,0:T(8,128)S(1)} %broadcast_multiply_fusion.4), kind=kLoop, calls=%fused_computation.1.clone.1 | loop fusion | flops 4259840 | bytes 9117696 | tf_op jit(solution)/shard_map/while/body/eval_jaxpr/mul | solution.py:30
  70.3 4.7 %fusion.29 = f32[64,8,2048]{2,1,0:T(8,128)S(1)} fusion(f32[64,8,2048]{2,1,0:T(8,128)S(1)} %copy-done, f32[65,8,2048]{2,1,0:T(8,128)S(1)} %fusion.26, f32[64,8,1]{2,1,0:T(8,128)S(1)} %get-tuple-element.131, f32[64,8,2047]{2,1,0:T(8,128)} %get-tuple-element.132, f32[64,8,2047]{2,1,0:T(8,128)S(1)} %copy-done.2, f32[64,8,1]{2,1,0:T(8,128)S(1)} %get-tuple-element.134, ...), kind=kLoop, calls=%fused_computation.4.clone.1 | loop fusion | flops 12582912 | bytes 26218496 | tf_op jit(solution)/shard_map/while/body/eval_jaxpr/add | solution.py:45
  75.0 2.0 copy-done.1
  77.9 1.9 collective-permute-start
  79.8 5.8 %collective-permute-start.1 = (f32[1,8,2048]{2,1,0:T(8,128)S(1)}, f32[1,8,2048]{2,1,0:T(8,128)S(1)}, u32[]{:S(2)}, u32[]{:S(2)}) collective-permute-start(f32[1,8,2048]{2,1,0:T(8,128)S(1)} %get-tuple-element.130), channel_id=1, source_target_pairs={{0,1},{1,2},{2,3},{3,4},{4,5},{5,6},{6,7},{7,8},{8,9},{9,10},{10,1... | collective-permute-start | bytes 196616 | tf_op jit(solution)/shard_map/while/body/eval_jaxpr/ppermute | solution.py:22
  85.6 8.1 %fusion.28 = (f32[64,8,2047]{2,1,0:T(8,128)}, f32[64,8,2047]{2,1,0:T(8,128)}) fusion(f32[64,8,2048]{2,1,0:T(8,128)} %get-tuple-element.147), kind=kLoop, calls=%fused_computation.37.clone.1 | loop fusion | bytes 16769024 | tf_op jit(solution)/shard_map/while/body/eval_jaxpr/jit(_roll_static)/slice | solution.py:41
  96.2 4.2 %fusion.26 = f32[65,8,2048]{2,1,0:T(8,128)S(1)} fusion(f32[1,8,2048]{2,1,0:T(8,128)S(1)} %collective-permute-done, f32[64,8,2048]{2,1,0:T(8,128)} %get-tuple-element.147, f32[1,8,2048]{2,1,0:T(8,128)S(1)} %collective-permute-done.1, f32[65,2048]{1,0:T(8,128)S(1)} %broadcast_multiply_fusion.4), kind=kLoop, calls=%fused_computation.1.clone.1 | loop fusion | flops 4259840 | bytes 9117696 | tf_op jit(solution)/shard_map/while/body/eval_jaxpr/mul | solution.py:30
  102.1 4.7 %fusion.29 = f32[64,8,2048]{2,1,0:T(8,128)S(1)} fusion(f32[64,8,2048]{2,1,0:T(8,128)S(1)} %copy-done, f32[65,8,2048]{2,1,0:T(8,128)S(1)} %fusion.26, f32[64,8,1]{2,1,0:T(8,128)S(1)} %get-tuple-element.131, f32[64,8,2047]{2,1,0:T(8,128)} %get-tuple-element.132, f32[64,8,2047]{2,1,0:T(8,128)S(1)} %copy-done.2, f32[64,8,1]{2,1,0:T(8,128)S(1)} %get-tuple-element.134, ...), kind=kLoop, calls=%fused_computation.4.clone.1 | loop fusion | flops 12582912 | bytes 26218496 | tf_op jit(solution)/shard_map/while/body/eval_jaxpr/add | solution.py:45
  106.8 2.0 copy-done.1
  109.7 1.9 collective-permute-start
  111.6 5.8 %collective-permute-start.1 = (f32[1,8,2048]{2,1,0:T(8,128)S(1)}, f32[1,8,2048]{2,1,0:T(8,128)S(1)}, u32[]{:S(2)}, u32[]{:S(2)}) collective-permute-start(f32[1,8,2048]{2,1,0:T(8,128)S(1)} %get-tuple-element.130), channel_id=1, source_target_pairs={{0,1},{1,2},{2,3},{3,4},{4,5},{5,6},{6,7},{7,8},{8,9},{9,10},{10,1... | collective-permute-start | bytes 196616 | tf_op jit(solution)/shard_map/while/body/eval_jaxpr/ppermute | solution.py:22
  117.4 8.1 %fusion.28 = (f32[64,8,2047]{2,1,0:T(8,128)}, f32[64,8,2047]{2,1,0:T(8,128)}) fusion(f32[64,8,2048]{2,1,0:T(8,128)} %get-tuple-element.147), kind=kLoop, calls=%fused_computation.37.clone.1 | loop fusion | bytes 16769024 | tf_op jit(solution)/shard_map/while/body/eval_jaxpr/jit(_roll_static)/slice | solution.py:41
  128.0 4.2 %fusion.26 = f32[65,8,2048]{2,1,0:T(8,128)S(1)} fusion(f32[1,8,2048]{2,1,0:T(8,128)S(1)} %collective-permute-done, f32[64,8,2048]{2,1,0:T(8,128)} %get-tuple-element.147, f32[1,8,2048]{2,1,0:T(8,128)S(1)} %collective-permute-done.1, f32[65,2048]{1,0:T(8,128)S(1)} %broadcast_multiply_fusion.4), kind=kLoop, calls=%fused_computation.1.clone.1 | loop fusion | flops 4259840 | bytes 9117696 | tf_op jit(solution)/shard_map/while/body/eval_jaxpr/mul | solution.py:30
  133.9 4.7 %fusion.29 = f32[64,8,2048]{2,1,0:T(8,128)S(1)} fusion(f32[64,8,2048]{2,1,0:T(8,128)S(1)} %copy-done, f32[65,8,2048]{2,1,0:T(8,128)S(1)} %fusion.26, f32[64,8,1]{2,1,0:T(8,128)S(1)} %get-tuple-element.131, f32[64,8,2047]{2,1,0:T(8,128)} %get-tuple-element.132, f32[64,8,2047]{2,1,0:T(8,128)S(1)} %copy-done.2, f32[64,8,1]{2,1,0:T(8,128)S(1)} %get-tuple-element.134, ...), kind=kLoop, calls=%fused_computation.4.clone.1 | loop fusion | flops 12582912 | bytes 26218496 | tf_op jit(solution)/shard_map/while/body/eval_jaxpr/add | solution.py:45
  138.6 2.0 copy-done.1
  141.5 1.9 collective-permute-start
  143.4 5.8 %collective-permute-start.1 = (f32[1,8,2048]{2,1,0:T(8,128)S(1)}, f32[1,8,2048]{2,1,0:T(8,128)S(1)}, u32[]{:S(2)}, u32[]{:S(2)}) collective-permute-start(f32[1,8,2048]{2,1,0:T(8,128)S(1)} %get-tuple-element.130), channel_id=1, source_target_pairs={{0,1},{1,2},{2,3},{3,4},{4,5},{5,6},{6,7},{7,8},{8,9},{9,10},{10,1... | collective-permute-start | bytes 196616 | tf_op jit(solution)/shard_map/while/body/eval_jaxpr/ppermute | solution.py:22
  149.2 8.1 %fusion.28 = (f32[64,8,2047]{2,1,0:T(8,128)}, f32[64,8,2047]{2,1,0:T(8,128)}) fusion(f32[64,8,2048]{2,1,0:T(8,128)} %get-tuple-element.147), kind=kLoop, calls=%fused_computation.37.clone.1 | loop fusion | bytes 16769024 | tf_op jit(solution)/shard_map/while/body/eval_jaxpr/jit(_roll_static)/slice | solution.py:41
  159.8 4.2 %fusion.26 = f32[65,8,2048]{2,1,0:T(8,128)S(1)} fusion(f32[1,8,2048]{2,1,0:T(8,128)S(1)} %collective-permute-done, f32[64,8,2048]{2,1,0:T(8,128)} %get-tuple-element.147, f32[1,8,2048]{2,1,0:T(8,128)S(1)} %collective-permute-done.1, f32[65,2048]{1,0:T(8,128)S(1)} %broadcast_multiply_fusion.4), kind=kLoop, calls=%fused_computation.1.clone.1 | loop fusion | flops 4259840 | bytes 9117696 | tf_op jit(solution)/shard_map/while/body/eval_jaxpr/mul | solution.py:30
  165.7 4.7 %fusion.29 = f32[64,8,2048]{2,1,0:T(8,128)S(1)} fusion(f32[64,8,2048]{2,1,0:T(8,128)S(1)} %copy-done, f32[65,8,2048]{2,1,0:T(8,128)S(1)} %fusion.26, f32[64,8,1]{2,1,0:T(8,128)S(1)} %get-tuple-element.131, f32[64,8,2047]{2,1,0:T(8,128)} %get-tuple-element.132, f32[64,8,2047]{2,1,0:T(8,128)S(1)} %copy-done.2, f32[64,8,1]{2,1,0:T(8,128)S(1)} %get-tuple-element.134, ...), kind=kLoop, calls=%fused_computation.4.clone.1 | loop fusion | flops 12582912 | bytes 26218496 | tf_op jit(solution)/shard_map/while/body/eval_jaxpr/add | solution.py:45
  170.4 2.0 copy-done.1
  173.3 1.9 collective-permute-start
  175.2 5.8 %collective-permute-start.1 = (f32[1,8,2048]{2,1,0:T(8,128)S(1)}, f32[1,8,2048]{2,1,0:T(8,128)S(1)}, u32[]{:S(2)}, u32[]{:S(2)}) collective-permute-start(f32[1,8,2048]{2,1,0:T(8,128)S(1)} %get-tuple-element.130), channel_id=1, source_target_pairs={{0,1},{1,2},{2,3},{3,4},{4,5},{5,6},{6,7},{7,8},{8,9},{9,10},{10,1... | collective-permute-start | bytes 196616 | tf_op jit(solution)/shard_map/while/body/eval_jaxpr/ppermute | solution.py:22
  181.0 8.1 %fusion.28 = (f32[64,8,2047]{2,1,0:T(8,128)}, f32[64,8,2047]{2,1,0:T(8,128)}) fusion(f32[64,8,2048]{2,1,0:T(8,128)} %get-tuple-element.147), kind=kLoop, calls=%fused_computation.37.clone.1 | loop fusion | bytes 16769024 | tf_op jit(solution)/shard_map/while/body/eval_jaxpr/jit(_roll_static)/slice | solution.py:41
  191.6 4.2 %fusion.26 = f32[65,8,2048]{2,1,0:T(8,128)S(1)} fusion(f32[1,8,2048]{2,1,0:T(8,128)S(1)} %collective-permute-done, f32[64,8,2048]{2,1,0:T(8,128)} %get-tuple-element.147, f32[1,8,2048]{2,1,0:T(8,128)S(1)} %collective-permute-done.1, f32[65,2048]{1,0:T(8,128)S(1)} %broadcast_multiply_fusion.4), kind=kLoop, calls=%fused_computation.1.clone.1 | loop fusion | flops 4259840 | bytes 9117696 | tf_op jit(solution)/shard_map/while/body/eval_jaxpr/mul | solution.py:30
  197.4 4.7 %fusion.29 = f32[64,8,2048]{2,1,0:T(8,128)S(1)} fusion(f32[64,8,2048]{2,1,0:T(8,128)S(1)} %copy-done, f32[65,8,2048]{2,1,0:T(8,128)S(1)} %fusion.26, f32[64,8,1]{2,1,0:T(8,128)S(1)} %get-tuple-element.131, f32[64,8,2047]{2,1,0:T(8,128)} %get-tuple-element.132, f32[64,8,2047]{2,1,0:T(8,128)S(1)} %copy-done.2, f32[64,8,1]{2,1,0:T(8,128)S(1)} %get-tuple-element.134, ...), kind=kLoop, calls=%fused_computation.4.clone.1 | loop fusion | flops 12582912 | bytes 26218496 | tf_op jit(solution)/shard_map/while/body/eval_jaxpr/add | solution.py:45
  202.2 2.0 copy-done.1
  205.1 1.9 collective-permute-start
  207.0 5.8 %collective-permute-start.1 = (f32[1,8,2048]{2,1,0:T(8,128)S(1)}, f32[1,8,2048]{2,1,0:T(8,128)S(1)}, u32[]{:S(2)}, u32[]{:S(2)}) collective-permute-start(f32[1,8,2048]{2,1,0:T(8,128)S(1)} %get-tuple-element.130), channel_id=1, source_target_pairs={{0,1},{1,2},{2,3},{3,4},{4,5},{5,6},{6,7},{7,8},{8,9},{9,10},{10,1... | collective-permute-start | bytes 196616 | tf_op jit(solution)/shard_map/while/body/eval_jaxpr/ppermute | solution.py:22
  212.8 8.1 %fusion.28 = (f32[64,8,2047]{2,1,0:T(8,128)}, f32[64,8,2047]{2,1,0:T(8,128)}) fusion(f32[64,8,2048]{2,1,0:T(8,128)} %get-tuple-element.147), kind=kLoop, calls=%fused_computation.37.clone.1 | loop fusion | bytes 16769024 | tf_op jit(solution)/shard_map/while/body/eval_jaxpr/jit(_roll_static)/slice | solution.py:41
  223.3 4.2 %fusion.26 = f32[65,8,2048]{2,1,0:T(8,128)S(1)} fusion(f32[1,8,2048]{2,1,0:T(8,128)S(1)} %collective-permute-done, f32[64,8,2048]{2,1,0:T(8,128)} %get-tuple-element.147, f32[1,8,2048]{2,1,0:T(8,128)S(1)} %collective-permute-done.1, f32[65,2048]{1,0:T(8,128)S(1)} %broadcast_multiply_fusion.4), kind=kLoop, calls=%fused_computation.1.clone.1 | loop fusion | flops 4259840 | bytes 9117696 | tf_op jit(solution)/shard_map/while/body/eval_jaxpr/mul | solution.py:30
  229.2 4.7 %fusion.29 = f32[64,8,2048]{2,1,0:T(8,128)S(1)} fusion(f32[64,8,2048]{2,1,0:T(8,128)S(1)} %copy-done, f32[65,8,2048]{2,1,0:T(8,128)S(1)} %fusion.26, f32[64,8,1]{2,1,0:T(8,128)S(1)} %get-tuple-element.131, f32[64,8,2047]{2,1,0:T(8,128)} %get-tuple-element.132, f32[64,8,2047]{2,1,0:T(8,128)S(1)} %copy-done.2, f32[64,8,1]{2,1,0:T(8,128)S(1)} %get-tuple-element.134, ...), kind=kLoop, calls=%fused_computation.4.clone.1 | loop fusion | flops 12582912 | bytes 26218496 | tf_op jit(solution)/shard_map/while/body/eval_jaxpr/add | solution.py:45
  234.0 2.0 copy-done.1
  (107 shorter events, 35.2 us)
Async XLA Ops:
  0.0 27.3 %copy-start.5 = (f32[64,2048]{1,0:T(8,128)S(1)}, f32[64,2048]{1,0:T(8,128)}, u32[]{:S(2)}) copy-start(f32[64,2048]{1,0:T(8,128)} %param.8) | copy-start | bytes 1572868
  0.0 27.6 %copy-start.7 = (f32[8]{0:T(128)S(1)}, f32[8]{0:T(128)}, u32[]{:S(2)}) copy-start(f32[8]{0:T(128)} %param.11) | copy-start | bytes 100
  0.0 27.6 %copy-start.3 = (f32[64,8,2048]{2,1,0:T(8,128)S(1)}, f32[64,8,2048]{2,1,0:T(8,128)}, u32[]{:S(2)}) copy-start(f32[64,8,2048]{2,1,0:T(8,128)} %param.7) | copy-start | bytes 12582916
  0.0 27.6 %copy-start.6 = (f32[8]{0:T(128)S(1)}, f32[8]{0:T(128)}, u32[]{:S(2)}) copy-start(f32[8]{0:T(128)} %param.10) | copy-start | bytes 100
  1.1 35.9 %collective-permute-start.4 = (f32[6,2048]{1,0:T(8,128)S(1)}, f32[6,2048]{1,0:T(8,128)S(1)}, u32[]{:S(2)}, u32[]{:S(2)}) collective-permute-start(f32[6,2048]{1,0:T(8,128)S(1)} %get-tuple-element.76), channel_id=1, source_target_pairs={{1,0},{2,1},{3,2},{4,3},{5,4},{6,5},{7,6},{8,7},{9,8},{10,9},{11,1... | collective-permute-start | bytes 147464 | tf_op jit(solution)/shard_map/ppermute | solution.py:23
  3.8 33.2 %collective-permute-start.5 = (f32[6,2048]{1,0:T(8,128)S(1)}, f32[6,2048]{1,0:T(8,128)S(1)}, u32[]{:S(2)}, u32[]{:S(2)}) collective-permute-start(f32[6,2048]{1,0:T(8,128)S(1)} %get-tuple-element.77), channel_id=1, source_target_pairs={{0,1},{1,2},{2,3},{3,4},{4,5},{5,6},{6,7},{7,8},{8,9},{9,10},{10,1... | collective-permute-start | bytes 147464 | tf_op jit(solution)/shard_map/ppermute | solution.py:22
  16.3 21.7 %collective-permute-start.3 = (f32[64,2048]{1,0:T(8,128)}, f32[64,2048]{1,0:T(8,128)S(1)}, u32[]{:S(2)}, u32[]{:S(2)}) collective-permute-start(f32[64,2048]{1,0:T(8,128)} %fusion.11), channel_id=1, source_target_pairs={{0,16},{16,32},{32,48},{48,64},{64,80},{80,96},{96,112},{112,128},... | collective-permute-start | bytes 1572872 | tf_op jit(solution)/shard_map/ppermute | solution.py:12
  21.5 16.6 %collective-permute-start.2 = (f32[64,2048]{1,0:T(8,128)}, f32[64,2048]{1,0:T(8,128)}, u32[]{:S(2)}, u32[]{:S(2)}) collective-permute-start(f32[64,2048]{1,0:T(8,128)} %fusion.12), channel_id=1, source_target_pairs={{16,0},{32,16},{48,32},{64,48},{80,64},{96,80},{112,96},{128,112},... | collective-permute-start | bytes 1572872 | tf_op jit(solution)/shard_map/ppermute | solution.py:12
  31.7 6.3 %copy-start.8 = (f32[8]{0:T(128)S(1)}, f32[8]{0:T(128)}, u32[]{:S(2)}) copy-start(f32[8]{0:T(128)} %param.9) | copy-start | bytes 100
  46.1 18.3 %collective-permute-start = (f32[1,8,2048]{2,1,0:T(8,128)S(1)}, f32[1,8,2048]{2,1,0:T(8,128)S(1)}, u32[]{:S(2)}, u32[]{:S(2)}) collective-permute-start(f32[1,8,2048]{2,1,0:T(8,128)S(1)} %get-tuple-element.129), channel_id=1, source_target_pairs={{1,0},{2,1},{3,2},{4,3},{5,4},{6,5},{7,6},{8,7},{9,8},{10,9},{11,1... | collective-permute-start | bytes 196616 | tf_op jit(solution)/shard_map/while/body/eval_jaxpr/ppermute | solution.py:23
  48.1 16.3 %collective-permute-start.1 = (f32[1,8,2048]{2,1,0:T(8,128)S(1)}, f32[1,8,2048]{2,1,0:T(8,128)S(1)}, u32[]{:S(2)}, u32[]{:S(2)}) collective-permute-start(f32[1,8,2048]{2,1,0:T(8,128)S(1)} %get-tuple-element.130), channel_id=1, source_target_pairs={{0,1},{1,2},{2,3},{3,4},{4,5},{5,6},{6,7},{7,8},{8,9},{9,10},{10,1... | collective-permute-start | bytes 196616 | tf_op jit(solution)/shard_map/while/body/eval_jaxpr/ppermute | solution.py:22
  53.8 8.1 %copy-start.4 = (f32[66,2048]{1,0:T(8,128)S(1)}, f32[66,2048]{1,0:T(8,128)}, u32[]{:S(2)}) copy-start(f32[66,2048]{1,0:T(8,128)} %get-tuple-element.156) | copy-start | bytes 1622020 | tf_op jit(solution)/shard_map/while
  64.4 4.7 %copy-start = (f32[64,8,2048]{2,1,0:T(8,128)S(1)}, f32[64,8,2048]{2,1,0:T(8,128)}, u32[]{:S(2)}) copy-start(f32[64,8,2048]{2,1,0:T(8,128)} %get-tuple-element.147) | copy-start | bytes 12582916 | tf_op jit(solution)/shard_map/while
  64.4 5.9 %copy-start.2 = (f32[64,8,2047]{2,1,0:T(8,128)S(1)}, f32[64,8,2047]{2,1,0:T(8,128)}, u32[]{:S(2)}) copy-start(f32[64,8,2047]{2,1,0:T(8,128)} %get-tuple-element.133) | copy-start | bytes 12576772 | tf_op jit(solution)/shard_map/while
  75.0 2.0 copy-start.1
  77.9 18.3 %collective-permute-start = (f32[1,8,2048]{2,1,0:T(8,128)S(1)}, f32[1,8,2048]{2,1,0:T(8,128)S(1)}, u32[]{:S(2)}, u32[]{:S(2)}) collective-permute-start(f32[1,8,2048]{2,1,0:T(8,128)S(1)} %get-tuple-element.129), channel_id=1, source_target_pairs={{1,0},{2,1},{3,2},{4,3},{5,4},{6,5},{7,6},{8,7},{9,8},{10,9},{11,1... | collective-permute-start | bytes 196616 | tf_op jit(solution)/shard_map/while/body/eval_jaxpr/ppermute | solution.py:23
  79.8 16.3 %collective-permute-start.1 = (f32[1,8,2048]{2,1,0:T(8,128)S(1)}, f32[1,8,2048]{2,1,0:T(8,128)S(1)}, u32[]{:S(2)}, u32[]{:S(2)}) collective-permute-start(f32[1,8,2048]{2,1,0:T(8,128)S(1)} %get-tuple-element.130), channel_id=1, source_target_pairs={{0,1},{1,2},{2,3},{3,4},{4,5},{5,6},{6,7},{7,8},{8,9},{9,10},{10,1... | collective-permute-start | bytes 196616 | tf_op jit(solution)/shard_map/while/body/eval_jaxpr/ppermute | solution.py:22
  85.6 8.1 %copy-start.4 = (f32[66,2048]{1,0:T(8,128)S(1)}, f32[66,2048]{1,0:T(8,128)}, u32[]{:S(2)}) copy-start(f32[66,2048]{1,0:T(8,128)} %get-tuple-element.156) | copy-start | bytes 1622020 | tf_op jit(solution)/shard_map/while
  96.2 4.7 %copy-start = (f32[64,8,2048]{2,1,0:T(8,128)S(1)}, f32[64,8,2048]{2,1,0:T(8,128)}, u32[]{:S(2)}) copy-start(f32[64,8,2048]{2,1,0:T(8,128)} %get-tuple-element.147) | copy-start | bytes 12582916 | tf_op jit(solution)/shard_map/while
  96.2 5.9 %copy-start.2 = (f32[64,8,2047]{2,1,0:T(8,128)S(1)}, f32[64,8,2047]{2,1,0:T(8,128)}, u32[]{:S(2)}) copy-start(f32[64,8,2047]{2,1,0:T(8,128)} %get-tuple-element.133) | copy-start | bytes 12576772 | tf_op jit(solution)/shard_map/while
  106.8 2.0 copy-start.1
  109.7 18.3 %collective-permute-start = (f32[1,8,2048]{2,1,0:T(8,128)S(1)}, f32[1,8,2048]{2,1,0:T(8,128)S(1)}, u32[]{:S(2)}, u32[]{:S(2)}) collective-permute-start(f32[1,8,2048]{2,1,0:T(8,128)S(1)} %get-tuple-element.129), channel_id=1, source_target_pairs={{1,0},{2,1},{3,2},{4,3},{5,4},{6,5},{7,6},{8,7},{9,8},{10,9},{11,1... | collective-permute-start | bytes 196616 | tf_op jit(solution)/shard_map/while/body/eval_jaxpr/ppermute | solution.py:23
  111.6 16.3 %collective-permute-start.1 = (f32[1,8,2048]{2,1,0:T(8,128)S(1)}, f32[1,8,2048]{2,1,0:T(8,128)S(1)}, u32[]{:S(2)}, u32[]{:S(2)}) collective-permute-start(f32[1,8,2048]{2,1,0:T(8,128)S(1)} %get-tuple-element.130), channel_id=1, source_target_pairs={{0,1},{1,2},{2,3},{3,4},{4,5},{5,6},{6,7},{7,8},{8,9},{9,10},{10,1... | collective-permute-start | bytes 196616 | tf_op jit(solution)/shard_map/while/body/eval_jaxpr/ppermute | solution.py:22
  117.4 8.1 %copy-start.4 = (f32[66,2048]{1,0:T(8,128)S(1)}, f32[66,2048]{1,0:T(8,128)}, u32[]{:S(2)}) copy-start(f32[66,2048]{1,0:T(8,128)} %get-tuple-element.156) | copy-start | bytes 1622020 | tf_op jit(solution)/shard_map/while
  127.9 4.7 %copy-start = (f32[64,8,2048]{2,1,0:T(8,128)S(1)}, f32[64,8,2048]{2,1,0:T(8,128)}, u32[]{:S(2)}) copy-start(f32[64,8,2048]{2,1,0:T(8,128)} %get-tuple-element.147) | copy-start | bytes 12582916 | tf_op jit(solution)/shard_map/while
  128.0 5.9 %copy-start.2 = (f32[64,8,2047]{2,1,0:T(8,128)S(1)}, f32[64,8,2047]{2,1,0:T(8,128)}, u32[]{:S(2)}) copy-start(f32[64,8,2047]{2,1,0:T(8,128)} %get-tuple-element.133) | copy-start | bytes 12576772 | tf_op jit(solution)/shard_map/while
  138.6 2.0 copy-start.1
  141.5 18.3 %collective-permute-start = (f32[1,8,2048]{2,1,0:T(8,128)S(1)}, f32[1,8,2048]{2,1,0:T(8,128)S(1)}, u32[]{:S(2)}, u32[]{:S(2)}) collective-permute-start(f32[1,8,2048]{2,1,0:T(8,128)S(1)} %get-tuple-element.129), channel_id=1, source_target_pairs={{1,0},{2,1},{3,2},{4,3},{5,4},{6,5},{7,6},{8,7},{9,8},{10,9},{11,1... | collective-permute-start | bytes 196616 | tf_op jit(solution)/shard_map/while/body/eval_jaxpr/ppermute | solution.py:23
  143.4 16.3 %collective-permute-start.1 = (f32[1,8,2048]{2,1,0:T(8,128)S(1)}, f32[1,8,2048]{2,1,0:T(8,128)S(1)}, u32[]{:S(2)}, u32[]{:S(2)}) collective-permute-start(f32[1,8,2048]{2,1,0:T(8,128)S(1)} %get-tuple-element.130), channel_id=1, source_target_pairs={{0,1},{1,2},{2,3},{3,4},{4,5},{5,6},{6,7},{7,8},{8,9},{9,10},{10,1... | collective-permute-start | bytes 196616 | tf_op jit(solution)/shard_map/while/body/eval_jaxpr/ppermute | solution.py:22
  149.2 8.1 %copy-start.4 = (f32[66,2048]{1,0:T(8,128)S(1)}, f32[66,2048]{1,0:T(8,128)}, u32[]{:S(2)}) copy-start(f32[66,2048]{1,0:T(8,128)} %get-tuple-element.156) | copy-start | bytes 1622020 | tf_op jit(solution)/shard_map/while
  159.7 4.7 %copy-start = (f32[64,8,2048]{2,1,0:T(8,128)S(1)}, f32[64,8,2048]{2,1,0:T(8,128)}, u32[]{:S(2)}) copy-start(f32[64,8,2048]{2,1,0:T(8,128)} %get-tuple-element.147) | copy-start | bytes 12582916 | tf_op jit(solution)/shard_map/while
  159.7 5.9 %copy-start.2 = (f32[64,8,2047]{2,1,0:T(8,128)S(1)}, f32[64,8,2047]{2,1,0:T(8,128)}, u32[]{:S(2)}) copy-start(f32[64,8,2047]{2,1,0:T(8,128)} %get-tuple-element.133) | copy-start | bytes 12576772 | tf_op jit(solution)/shard_map/while
  170.4 2.0 copy-start.1
  173.3 18.3 %collective-permute-start = (f32[1,8,2048]{2,1,0:T(8,128)S(1)}, f32[1,8,2048]{2,1,0:T(8,128)S(1)}, u32[]{:S(2)}, u32[]{:S(2)}) collective-permute-start(f32[1,8,2048]{2,1,0:T(8,128)S(1)} %get-tuple-element.129), channel_id=1, source_target_pairs={{1,0},{2,1},{3,2},{4,3},{5,4},{6,5},{7,6},{8,7},{9,8},{10,9},{11,1... | collective-permute-start | bytes 196616 | tf_op jit(solution)/shard_map/while/body/eval_jaxpr/ppermute | solution.py:23
  175.2 16.3 %collective-permute-start.1 = (f32[1,8,2048]{2,1,0:T(8,128)S(1)}, f32[1,8,2048]{2,1,0:T(8,128)S(1)}, u32[]{:S(2)}, u32[]{:S(2)}) collective-permute-start(f32[1,8,2048]{2,1,0:T(8,128)S(1)} %get-tuple-element.130), channel_id=1, source_target_pairs={{0,1},{1,2},{2,3},{3,4},{4,5},{5,6},{6,7},{7,8},{8,9},{9,10},{10,1... | collective-permute-start | bytes 196616 | tf_op jit(solution)/shard_map/while/body/eval_jaxpr/ppermute | solution.py:22
  181.0 8.1 %copy-start.4 = (f32[66,2048]{1,0:T(8,128)S(1)}, f32[66,2048]{1,0:T(8,128)}, u32[]{:S(2)}) copy-start(f32[66,2048]{1,0:T(8,128)} %get-tuple-element.156) | copy-start | bytes 1622020 | tf_op jit(solution)/shard_map/while
  191.5 4.7 %copy-start = (f32[64,8,2048]{2,1,0:T(8,128)S(1)}, f32[64,8,2048]{2,1,0:T(8,128)}, u32[]{:S(2)}) copy-start(f32[64,8,2048]{2,1,0:T(8,128)} %get-tuple-element.147) | copy-start | bytes 12582916 | tf_op jit(solution)/shard_map/while
  191.5 5.9 %copy-start.2 = (f32[64,8,2047]{2,1,0:T(8,128)S(1)}, f32[64,8,2047]{2,1,0:T(8,128)}, u32[]{:S(2)}) copy-start(f32[64,8,2047]{2,1,0:T(8,128)} %get-tuple-element.133) | copy-start | bytes 12576772 | tf_op jit(solution)/shard_map/while
  202.2 2.0 copy-start.1
  205.1 18.3 %collective-permute-start = (f32[1,8,2048]{2,1,0:T(8,128)S(1)}, f32[1,8,2048]{2,1,0:T(8,128)S(1)}, u32[]{:S(2)}, u32[]{:S(2)}) collective-permute-start(f32[1,8,2048]{2,1,0:T(8,128)S(1)} %get-tuple-element.129), channel_id=1, source_target_pairs={{1,0},{2,1},{3,2},{4,3},{5,4},{6,5},{7,6},{8,7},{9,8},{10,9},{11,1... | collective-permute-start | bytes 196616 | tf_op jit(solution)/shard_map/while/body/eval_jaxpr/ppermute | solution.py:23
  207.0 16.3 %collective-permute-start.1 = (f32[1,8,2048]{2,1,0:T(8,128)S(1)}, f32[1,8,2048]{2,1,0:T(8,128)S(1)}, u32[]{:S(2)}, u32[]{:S(2)}) collective-permute-start(f32[1,8,2048]{2,1,0:T(8,128)S(1)} %get-tuple-element.130), channel_id=1, source_target_pairs={{0,1},{1,2},{2,3},{3,4},{4,5},{5,6},{6,7},{7,8},{8,9},{9,10},{10,1... | collective-permute-start | bytes 196616 | tf_op jit(solution)/shard_map/while/body/eval_jaxpr/ppermute | solution.py:22
  212.8 8.1 %copy-start.4 = (f32[66,2048]{1,0:T(8,128)S(1)}, f32[66,2048]{1,0:T(8,128)}, u32[]{:S(2)}) copy-start(f32[66,2048]{1,0:T(8,128)} %get-tuple-element.156) | copy-start | bytes 1622020 | tf_op jit(solution)/shard_map/while
  223.3 4.7 %copy-start = (f32[64,8,2048]{2,1,0:T(8,128)S(1)}, f32[64,8,2048]{2,1,0:T(8,128)}, u32[]{:S(2)}) copy-start(f32[64,8,2048]{2,1,0:T(8,128)} %get-tuple-element.147) | copy-start | bytes 12582916 | tf_op jit(solution)/shard_map/while
  223.3 5.9 %copy-start.2 = (f32[64,8,2047]{2,1,0:T(8,128)S(1)}, f32[64,8,2047]{2,1,0:T(8,128)}, u32[]{:S(2)}) copy-start(f32[64,8,2047]{2,1,0:T(8,128)} %get-tuple-element.133) | copy-start | bytes 12576772 | tf_op jit(solution)/shard_map/while
  233.9 2.0 copy-start.1
where the time goes:
time: 237 us; the launch traced here: 236 us
  local copies, waits for them, and re-layouts  95.6 us (40%)
  other arithmetic  76.3 us (32%)
  starting transfers between devices  63.2 us (27%)
    slice x12, local copies, waits for them, and re-layouts, single_diffusion_step(): jnp.roll(interior_slice, 1, axis=-1)  55.4 us
    ppermute x7, starting transfers between devices, padded(): before = lax.ppermute(last, axis, up)  39.6 us
    add x6, other arithmetic, single_diffusion_step(): return interior_slice + div_rows + div_cols  28.2 us
    mul x6, other arithmetic, single_diffusion_step(): interface_rows[:, None, :] * (value_extended[1:] - value_extended[:-1])  25.2 us
    while x48, local copies, waits for them, and re-layouts  22.3 us
    ppermute x7, starting transfers between devices, padded(): after = lax.ppermute(initial, axis, down)  14.2 us
    ppermute x2, starting transfers between devices, passed_along(): lax.ppermute(value, axis, [(source, source + steps) for source in range(i...  9.32 us
    mul x6, other arithmetic, single_diffusion_step(): east_face = (0.5 * (kin + k_east))[:, None, :]  7.34 us
  transfers between devices with their start and end apart: 16, of which 0 were waited for; matrix products, arithmetic and copies ran while one was open for 35% of the time, Pallas kernels for 0%

commit v1 on v0

v1 whole, which is shorter than its diff:
```python
import functools

import jax
import jax.numpy as jnp
from jax import lax
from jax.experimental import pallas as pl
from jax.experimental.pallas import tpu as pltpu
from jax.sharding import PartitionSpec as P

STEPS = 6
NV = 16
GV = NV + 2
LANES = 128
TILE = (8, LANES)
VMEM_LIMIT = 56 * 2**20
F32 = jnp.float32


def iota(dim):
    return lax.broadcasted_iota(jnp.int32, TILE, dim)


def to_columns(rows, scratch):
    scratch[...] = jnp.concatenate(rows, axis=0).T
    return [scratch[pl.ds(i, 8, stride=NV), :] for i in range(NV)]


def to_rows(columns, scratch):
    for i in range(NV):
        scratch[pl.ds(i, 8, stride=NV), :] = columns[i]
    flipped = scratch[...].T
    return [flipped[8 * j : 8 * j + 8] for j in range(NV)]


def ghost_west(last):
    turned = pltpu.roll(last, 1, 0)
    moved = jnp.where(iota(1) >= 8, pltpu.roll(turned, 8, 1), 0.0)
    return jnp.where(iota(0) == 0, moved, turned)


def ghost_east(first):
    turned = pltpu.roll(first, 7, 0)
    moved = jnp.where(iota(1) < LANES - 8, pltpu.roll(turned, LANES - 8, 1), 0.0)
    return jnp.where(iota(0) == 7, moved, turned)


def put_row(buffer, row, columns):
    for i in range(NV):
        buffer[row, i + 1] = columns[i]
    buffer[row, 0] = ghost_west(columns[NV - 1])
    buffer[row, NV + 1] = ghost_east(columns[0])


def mix_row(coef, row, field, before, after):
    slot = iota(0)
    mixed = []
    for j in range(NV):
        at = pl.ds(LANES * j, LANES)
        x = field[row, :, at]
        later = coef[1] * pltpu.roll(x, 7, 0)
        earlier = coef[2] * pltpu.roll(x, 1, 0)
        later = jnp.where(slot == 7, jnp.broadcast_to(after[row, :, at], TILE), later)
        earlier = jnp.where(slot == 0, jnp.broadcast_to(before[row, :, at], TILE), earlier)
        mixed.append(coef[0] * x + later + earlier)
    return mixed


def diffuse(src, dst, east, south, lo, count, shift=0, unroll=2, scale=None):
    def row_of(buffer, row):
        return [buffer[row, i + 1] for i in range(NV)]

    def finish(row, first, last):
        dst[row, 0] = ghost_west(last)
        dst[row, NV + 1] = ghost_east(first)

    def body(k, carry):
        row = lo + k
        v, north, (first, last) = carry[:NV], carry[NV : 2 * NV], carry[2 * NV :]
        finish(jnp.maximum(row - 1, lo), first, last)
        below = row_of(src, row + 1)
        west = east[row + shift, 0] * (v[0] - src[row, 0])
        new, flux = [], []
        for i in range(NV):
            v_east = v[i + 1] if i + 1 < NV else src[row, NV + 1]
            here = east[row + shift, i + 1] * (v_east - v[i])
            under = south[row + shift, i] * (below[i] - v[i])
            value = (v[i] + (here - west)) + (under - north[i])
            if scale is not None:
                value = value * scale(row)
            dst[row, i + 1] = value
            west = here
            flux.append(under)
            if i in (0, NV - 1):
                new.append(value)
        return (*below, *flux, *new)

    above, v = row_of(src, lo - 1), row_of(src, lo)
    north = [south[lo - 1 + shift, i] * (v[i] - above[i]) for i in range(NV)]
    out = lax.fori_loop(0, count, body, (*v, *north, v[0], v[NV - 1]), unroll=unroll)
    finish(lo + count - 1, *out[2 * NV :])


def coefficient_rows(half, east, south, lo, count, shift=0):
    def body(k, carry):
        row = lo + k
        here = [half[row, i] for i in range(GV)]
        for i in range(NV + 1):
            east[row + shift, i] = here[i] + here[i + 1]
        for i in range(NV):
            south[row + shift, i] = here[i + 1] + half[row + 1, i + 1]
        return carry

    lax.fori_loop(0, count, body, 0)


def faces_kernel(kappa, east, south, half, scratch):
    rows = kappa.shape[0]

    def block(b, carry):
        base = pl.multiple_of(b * 8, 8)
        part = kappa.at[pl.ds(base, 8), :]
        for q in range(8):
            spread = [jnp.broadcast_to(0.5 * part[q : q + 1, LANES * j : LANES * (j + 1)], TILE) for j in range(NV)]
            put_row(half, b * 8 + q, to_columns(spread, scratch.at[q]))
        return carry

    lax.fori_loop(0, rows // 8, block, 0)
    for i in range(GV):
        half[rows, i] = jnp.zeros(TILE, F32)
    coefficient_rows(half, east, south, 0, rows)


def faces(kappa):
    rows = kappa.shape[0]
    vmem = pl.BlockSpec(memory_space=pltpu.VMEM)
    return pl.pallas_call(
        faces_kernel,
        out_shape=(
            jax.ShapeDtypeStruct((rows, NV + 1, *TILE), F32),
            jax.ShapeDtypeStruct((rows, NV, *TILE), F32),
        ),
        in_specs=[vmem],
        out_specs=(vmem, vmem),
        scratch_shapes=[pltpu.VMEM((rows + 1, GV, *TILE), F32), pltpu.VMEM((8, LANES, LANES), F32)],
        compiler_params=pltpu.CompilerParams(vmem_limit_bytes=VMEM_LIMIT),
        cost_estimate=pl.CostEstimate(flops=10**7, bytes_accessed=9 * 2**20, transcendentals=0),
        name="faces",
    )(kappa)


def edges_kernel(coef, field_top, field_bottom, before, after, kappa_top, kappa_bottom, to_up, to_down):
    rows = before.shape[0]
    for side, field, kappa, start, out in ((0, field_top, kappa_top, 0, to_up), (1, field_bottom, kappa_bottom, rows - 8, to_down)):
        for k in range(STEPS):
            row = k if side == 0 else 2 + k
            mixed = mix_row(coef, row, field, before.at[pl.ds(start, 8)], after.at[pl.ds(start, 8)])
            for j in range(NV):
                out[k, :, pl.ds(LANES * j, LANES)] = mixed[j]
        out[STEPS] = kappa[...]


def edge_rows(coef, fields, before, after, kappa):
    rows, slots, width = fields.shape
    full = lambda shape: pl.BlockSpec(shape, lambda _: (0,) * len(shape))
    top, bottom = (lambda _: (0, 0, 0)), (lambda _: (rows // 8 - 1, 0, 0))
    out = jax.ShapeDtypeStruct((STEPS + 1, slots, width), F32)
    return pl.pallas_call(
        edges_kernel,
        grid=(1,),
        out_shape=(out, out),
        in_specs=[
            full(coef.shape),
            pl.BlockSpec((8, slots, width), top),
            pl.BlockSpec((8, slots, width), bottom),
            full(before.shape),
            full(after.shape),
            pl.BlockSpec((8, width), lambda _: (0, 0)),
            pl.BlockSpec((8, width), lambda _: (rows // 8 - 1, 0)),
        ],
        out_specs=(full(out.shape), full(out.shape)),
        compiler_params=pltpu.CompilerParams(vmem_limit_bytes=VMEM_LIMIT),
        cost_estimate=pl.CostEstimate(flops=10**6, bytes_accessed=3 * 2**20, transcendentals=0),
        name="edges",
    )(coef, fields, fields, before, after, kappa, kappa)


KEEP = STEPS + 1


def inner_kernel(coef, field, before, after, east_hbm, south_hbm, result, kept, field_v, east, south, one, two, scratch, sems):
    rows = field.shape[0]
    n_blocks = rows // 8
    loads = [pltpu.make_async_copy(field.at[pl.ds(8 * b, 8)], field_v.at[pl.ds(8 * b, 8)], sems.at[b]) for b in range(n_blocks)]
    faces_in = [pltpu.make_async_copy(east_hbm, east, sems.at[n_blocks]), pltpu.make_async_copy(south_hbm, south, sems.at[n_blocks + 1])]
    for copy in (*loads, *faces_in):
        copy.start()

    def block(b, carry):
        for q in range(8):
            row = b * 8 + q
            put_row(one, row, to_columns(mix_row(coef, row, field_v, before, after), scratch.at[q]))
        return carry

    for b in range(n_blocks):
        loads[b].wait()
    lax.fori_loop(0, n_blocks, block, 0)
    for copy in faces_in:
        copy.wait()
    for step in range(1, STEPS + 1):
        src, dst = (one, two) if step % 2 else (two, one)
        diffuse(src, dst, east, south, step, rows - 2 * step)
    last = one if STEPS % 2 == 0 else two

    keeps = [
        pltpu.make_async_copy(buffer.at[pl.ds(start, KEEP)], kept.at[at], sems.at[at])
        for at, (buffer, start) in enumerate(((one, 0), (two, 0), (one, rows - KEEP), (two, rows - KEEP)))
    ]
    for copy in keeps:
        copy.start()

    def back(b, carry):
        for q in range(8):
            row = b * 8 + q
            out = to_rows([last[row, i + 1] for i in range(NV)], scratch.at[q])
            for j in range(NV):
                field_v[row, :, pl.ds(LANES * j, LANES)] = out[j]
        return carry

    lax.fori_loop(0, n_blocks, back, 0)
    store = pltpu.make_async_copy(field_v.at[pl.ds(STEPS, rows - 2 * STEPS)], result.at[pl.ds(STEPS, rows - 2 * STEPS)], sems.at[4])
    store.start()
    for copy in (*keeps, store):
        copy.wait()


def inner(coef, fields, before, after, east, south):
    rows, slots, width = fields.shape
    vmem, hbm = pl.BlockSpec(memory_space=pltpu.VMEM), pl.BlockSpec(memory_space=pl.ANY)
    return pl.pallas_call(
        inner_kernel,
        out_shape=(
            jax.ShapeDtypeStruct(fields.shape, F32),
            jax.ShapeDtypeStruct((4, KEEP, GV, *TILE), F32),
        ),
        in_specs=[vmem, hbm, vmem, vmem, hbm, hbm],
        out_specs=(hbm, hbm),
        scratch_shapes=[
            pltpu.VMEM(fields.shape, F32),
            pltpu.VMEM(east.shape, F32),
            pltpu.VMEM(south.shape, F32),
            pltpu.VMEM((rows, GV, *TILE), F32),
            pltpu.VMEM((rows, GV, *TILE), F32),
            pltpu.VMEM((8, LANES, LANES), F32),
            pltpu.SemaphoreType.DMA((rows // 8 + 2,)),
        ],
        compiler_params=pltpu.CompilerParams(vmem_limit_bytes=VMEM_LIMIT),
        cost_estimate=pl.CostEstimate(flops=10**8, bytes_accessed=20 * 2**20, transcendentals=0),
        name="inner",
    )(coef, fields, before, after, east, south)


SPAN = 2 * STEPS + 1


def ends_kernel(inside, from_up, from_down, kappa_up, kappa_down, kept, east_hbm, south_hbm, partial, result, one, two, half, east, south, scratch, staged, sems):
    del partial
    rows = result.shape[0]
    upper, lower = 0, 1
    kept_in, faces_in = [], []
    for side in (upper, lower):
        own = STEPS if side == upper else 0
        first = 0 if side == upper else rows - KEEP
        pairs = ((kept.at[2 * side], one), (kept.at[2 * side + 1], two), (east_hbm.at[pl.ds(first, KEEP)], east), (south_hbm.at[pl.ds(first, KEEP)], south))
        for at, (src, dst) in enumerate(pairs):
            copy = pltpu.make_async_copy(src, dst.at[side, pl.ds(own, KEEP)], sems.at[4 * side + at])
            copy.start()
            (kept_in if at < 2 else faces_in).append(copy)
    for copy in (*kept_in, *faces_in):
        copy.wait()

    for side, halo, own_kappa in ((upper, from_up, kappa_up), (lower, from_down, kappa_down)):
        start = 0 if side == upper else KEEP
        for k in range(STEPS):
            put_row(one.at[side], start + k, to_columns([inside[side] * halo[k, :, pl.ds(LANES * j, LANES)] for j in range(NV)], scratch.at[k]))
        for k in range(STEPS + 1):
            is_own = k == STEPS if side == upper else k == 0
            if is_own:
                source, q = (own_kappa, 0) if side == upper else (own_kappa, 7)
            else:
                source, q = halo.at[STEPS], (k + 2 if side == upper else k - 1)
            factor = 0.5 if is_own else 0.5 * inside[side]
            spread = [jnp.broadcast_to(factor * source[q : q + 1, LANES * j : LANES * (j + 1)], TILE) for j in range(NV)]
            put_row(half, k, to_columns(spread, scratch.at[k]))
        if side == upper:
            coefficient_rows(half, east.at[side], south.at[side], 0, STEPS)
        else:
            for i in range(GV):
                half[STEPS + 1, i] = jnp.zeros(TILE, F32)
            for i in range(NV):
                south[side, STEPS, i] = half[0, i + 1] + half[1, i + 1]
            coefficient_rows(half, east.at[side], south.at[side], 1, STEPS, shift=STEPS)

    for step in range(1, STEPS + 1):
        src, dst = (one, two) if step % 2 else (two, one)
        keep_up, keep_down = inside[0], inside[1]
        diffuse(src.at[upper], dst.at[upper], east.at[upper], south.at[upper], step, STEPS, scale=lambda row: jnp.where(row < STEPS, keep_up, 1.0))
        diffuse(src.at[lower], dst.at[lower], east.at[lower], south.at[lower], SPAN - 1 - step - STEPS + 1, STEPS, scale=lambda row: jnp.where(row > STEPS, keep_down, 1.0))
    last = one if STEPS % 2 == 0 else two
    stores = []
    for side in (upper, lower):
        start = STEPS if side == upper else 1
        for k in range(STEPS):
            out = to_rows([last[side, start + k, i + 1] for i in range(NV)], scratch.at[k])
            for j in range(NV):
                staged[side, k, :, pl.ds(LANES * j, LANES)] = out[j]
        copy = pltpu.make_async_copy(staged.at[side], result.at[pl.ds(0 if side == upper else rows - STEPS, STEPS)], sems.at[side])
        copy.start()
        stores.append(copy)
    for copy in stores:
        copy.wait()


def ends(inside, from_up, from_down, kappa, kept, east, south, partial):
    rows, slots, width = partial.shape
    vmem, hbm = pl.BlockSpec(memory_space=pltpu.VMEM), pl.BlockSpec(memory_space=pl.ANY)
    return pl.pallas_call(
        ends_kernel,
        grid=(1,),
        out_shape=jax.ShapeDtypeStruct(partial.shape, F32),
        in_specs=[
            pl.BlockSpec(memory_space=pltpu.SMEM),
            vmem,
            vmem,
            pl.BlockSpec((8, width), lambda _: (0, 0)),
            pl.BlockSpec((8, width), lambda _: (rows // 8 - 1, 0)),
            hbm,
            hbm,
            hbm,
            hbm,
        ],
        out_specs=hbm,
        scratch_shapes=[
            pltpu.VMEM((2, SPAN, GV, *TILE), F32),
            pltpu.VMEM((2, SPAN, GV, *TILE), F32),
            pltpu.VMEM((STEPS + 2, GV, *TILE), F32),
            pltpu.VMEM((2, SPAN, NV + 1, *TILE), F32),
            pltpu.VMEM((2, SPAN, NV, *TILE), F32),
            pltpu.VMEM((8, LANES, LANES), F32),
            pltpu.VMEM((2, STEPS, slots, width), F32),
            pltpu.SemaphoreType.DMA((8,)),
        ],
        input_output_aliases={8: 0},
        compiler_params=pltpu.CompilerParams(vmem_limit_bytes=VMEM_LIMIT),
        cost_estimate=pl.CostEstimate(flops=10**7, bytes_accessed=8 * 2**20, transcendentals=0),
        name="ends",
    )(inside, from_up, from_down, kappa, kappa, kept, east, south, partial)


def ring(axis, step):
    size = lax.axis_size(axis)
    return [(i, (i + step) % size) for i in range(size)]


def local(forcing, kappa, diag_coef, lower_coef, upper_coef):
    slots = forcing.shape[1]
    tm, space = lax.axis_index("tm"), lax.axis_index("space")
    n_tm, n_space = lax.axis_size("tm"), lax.axis_size("space")
    down = jnp.where(tm == 0, 0.0, lower_coef[0]) * forcing[:, :1]
    up = jnp.where(tm == n_tm - 1, 0.0, upper_coef[slots - 1]) * forcing[:, slots - 1 :]
    after = lax.ppermute(down, "tm", ring("tm", -1))
    before = lax.ppermute(up, "tm", ring("tm", 1))
    east, south = faces(kappa)

    none = jnp.zeros((1,), F32)
    coef = jnp.stack([diag_coef, jnp.concatenate([lower_coef[1:], none]), jnp.concatenate([none, upper_coef[:-1]])])
    coef = jnp.broadcast_to(coef[:, :, None], (3, slots, LANES))
    inside = jnp.stack([jnp.where(space == 0, 0.0, 1.0), jnp.where(space == n_space - 1, 0.0, 1.0)]).astype(F32)

    to_up, to_down = edge_rows(coef, forcing, before, after, kappa)
    from_down = lax.ppermute(to_up, "space", ring("space", -1))
    from_up = lax.ppermute(to_down, "space", ring("space", 1))
    partial, kept = inner(coef, forcing, before, after, east, south)
    return ends(inside, from_up, from_down, kappa, kept, east, south, partial)


def solution(mesh):
    return jax.shard_map(
        local,
        mesh=mesh,
        in_specs=(P("space", "tm", None), P("space", None), P("tm"), P("tm"), P("tm")),
        out_specs=P("space", "tm", None),
        check_vma=False,
    )
```

time: 237 us -> 87.4 us (0.37)
  the two profiles are of different devices: /device:TPU:29 before, /device:TPU:2 now
where the time goes in v1:
time: 87.4 us; the launch traced here: 87.1 us
  Pallas kernels  49.3 us (56%)
  waiting for transfers between devices  14.9 us (17%)
  starting transfers between devices  11.4 us (13%)
  other arithmetic  6.62 us (8%)
  local copies, waits for them, and re-layouts  3.69 us (4%)
  between operations  1.36 us (2%)
    pallas_call x1, Pallas kernels, inner(): pl.pallas_call(inner_kernel, out_shape=(jax.ShapeDtypeStruct(fields.shape...  29.2 us
    pallas_call x1, Pallas kernels, ends(): pl.pallas_call(ends_kernel, grid=(1,), out_shape=jax.ShapeDtypeStruct(par...  9.4 us
    ppermute x1, waiting for transfers between devices, local(): after = lax.ppermute(down, 'tm', ring('tm', -1))  9.06 us
    pallas_call x1, Pallas kernels, faces(): pl.pallas_call(faces_kernel, out_shape=(jax.ShapeDtypeStruct((rows, NV +...  8.07 us
    ppermute x1, starting transfers between devices, local(): after = lax.ppermute(down, 'tm', ring('tm', -1))  7.49 us
    ppermute x1, waiting for transfers between devices, local(): before = lax.ppermute(up, 'tm', ring('tm', 1))  5.81 us
    mul x1, other arithmetic, local(): down = jnp.where(tm == 0, 0.0, lower_coef[0]) * forcing[:, :1]  4.56 us
    ppermute x1, starting transfers between devices, local(): from_down = lax.ppermute(to_up, 'space', ring('space', -1))  3.85 us
  transfers between devices with their start and end apart: 4, of which 2 were waited for; matrix products, arithmetic and copies ran while one was open for 3% of the time, Pallas kernels for 43%

profile of v1, /device:TPU:2, one launch (start us, length us, event | category | flops | bytes accessed | tf_op | source)
XLA Modules:
  0.0 87.1 jit_solution(7636165415402812056)
XLA Ops:
  0.0 1.2 %slice.20 = f32[1]{0:T(128)} slice(f32[8]{0:T(128)} %param.9), slice={[7:8]} | slice | bytes 8 | tf_op jit(solution)/shard_map/slice | solution.py:369
  2.5 4.6 %slice_multiply_fusion = (f32[64,1,2048]{2,1,0:T(1,128)S(1)}, f32[64,1,2048]{2,1,0:T(1,128)S(1)}) fusion(f32[64,8,2048]{2,1,0:T(8,128)} %field.1, f32[]{:T(128)S(6)} %select_n.17, f32[]{:T(128)S(6)} %select_n.16), kind=kLoop, calls=%fused_computation | loop fusion | flops 262144 | bytes 2097160 | tf_op jit(solution)/shard_map/mul | solution.py:368
  7.1 7.5 %collective-permute-start.1 = (f32[64,1,2048]{2,1,0:T(1,128)S(1)}, f32[64,1,2048]{2,1,0:T(1,128)S(1)}, u32[]{:S(2)}, u32[]{:S(2)}) collective-permute-start(f32[64,1,2048]{2,1,0:T(1,128)S(1)} %get-tuple-element.17), channel_id=1, source_target_pairs={{0,240},{16,0},{32,16},{48,32},{64,48},{80,64},{96,80},{112,96},{1... | collective-permute-start | bytes 1572872 | tf_op jit(solution)/shard_map/ppermute | solution.py:370
  14.6 0.0 collective-permute-start
  14.6 0.7 slice.18
  15.3 0.7 maximum_bitcast_fusion
  16.1 0.7 pad_maximum_fusion
  16.7 9.1 %collective-permute-done.1.after = f32[64,1,2048]{2,1,0:T(1,128)S(1)} collective-permute-done((f32[64,1,2048]{2,1,0:T(1,128)S(1)}, f32[64,1,2048]{2,1,0:T(1,128)S(1)}, u32[]{:S(2)}, u32[]{:S(2)}) %collective-permute-start.1) | collective-permute-done | bytes 524320 | tf_op jit(solution)/shard_map/ppermute | solution.py:370
  25.8 0.0 copy-start
  25.8 5.8 %collective-permute-done.before = f32[64,1,2048]{2,1,0:T(1,128)S(1)} collective-permute-done((f32[64,1,2048]{2,1,0:T(1,128)S(1)}, f32[64,1,2048]{2,1,0:T(1,128)S(1)}, u32[]{:S(2)}, u32[]{:S(2)}) %collective-permute-start) | collective-permute-done | bytes 524320 | tf_op jit(solution)/shard_map/ppermute | solution.py:371
  31.6 0.0 copy-start.1
  31.6 0.8 broadcast_in_dim.2.coef
  32.4 0.0 copy-done
  32.4 0.0 copy-done.1
  32.4 2.6 %edges.1 = (f32[7,8,2048]{2,1,0:T(8,128)}, f32[7,8,2048]{2,1,0:T(8,128)}) custom-call(f32[3,8,128]{2,1,0:T(8,128)} %broadcast_in_dim.2.coef, f32[64,8,2048]{2,1,0:T(8,128)} %field.1, f32[64,8,2048]{2,1,0:T(8,128)} %field.1, f32[64,1,2048]{2,1,0:T(1,128)} %copy-done.1, f32[64,1,2048]{2,1,0:T(1,128)} %copy-done, f32[64,2048]{1,0:T(8,128)} %kappa_down.1, ...), custom_call_target="tpu_custom_call" | custom-call | flops 1000000 | bytes 3145728 | tf_op jit(solution)/shard_map/edges/pallas_call | solution.py:167
  35.0 0.0 collective-permute-start.2
  35.0 3.9 %collective-permute-start.3 = (f32[7,8,2048]{2,1,0:T(8,128)}, f32[7,8,2048]{2,1,0:T(8,128)S(1)}, u32[]{:S(2)}, u32[]{:S(2)}) collective-permute-start(f32[7,8,2048]{2,1,0:T(8,128)} %get-tuple-element.12), channel_id=1, source_target_pairs={{0,15},{1,0},{2,1},{3,2},{4,3},{5,4},{6,5},{7,6},{8,7},{9,8},{10,9... | collective-permute-start | bytes 1376264 | tf_op jit(solution)/shard_map/ppermute | solution.py:380
  38.9 8.1 %faces.1 = (f32[64,17,8,128]{3,2,1,0:T(8,128)}, f32[64,16,8,128]{3,2,1,0:T(8,128)}) custom-call(f32[64,2048]{1,0:T(8,128)} %kappa_down.1), custom_call_target="tpu_custom_call" | custom-call | flops 10000000 | bytes 9437184 | tf_op jit(solution)/shard_map/faces/pallas_call | solution.py:136
  47.0 0.7 pad_maximum_fusion.1.inside
  47.6 29.2 %inner.1 = (f32[64,8,2048]{2,1,0:T(8,128)}, f32[4,7,18,8,128]{4,3,2,1,0:T(8,128)}) custom-call(f32[3,8,128]{2,1,0:T(8,128)} %broadcast_in_dim.2.coef, f32[64,8,2048]{2,1,0:T(8,128)} %field.1, f32[64,1,2048]{2,1,0:T(1,128)} %copy-done.1, f32[64,1,2048]{2,1,0:T(1,128)} %copy-done, f32[64,17,8,128]{3,2,1,0:T(8,128)} %get-tuple-element.13.east_hbm, ...), custom_call_target="tpu_custom_call" | custom-call | flops 100000000 | bytes 20971520 | tf_op jit(solution)/shard_map/inner/pallas_call | solution.py:239
  76.8 0.0 collective-permute-done.2.from_up
  76.8 0.0 copy-start.2
  76.8 0.0 collective-permute-done.3.from_down
  76.8 0.0 copy-start.3
  76.8 0.8 copy-done.2
  77.6 0.1 copy-done.3
  77.7 9.4 %ends.1 = f32[64,8,2048]{2,1,0:T(8,128)} custom-call(f32[2]{0:T(128)} %pad_maximum_fusion.1.inside, f32[7,8,2048]{2,1,0:T(8,128)} %copy-done.2, f32[7,8,2048]{2,1,0:T(8,128)} %copy-done.3, f32[64,2048]{1,0:T(8,128)} %kappa_down.1, f32[64,2048]{1,0:T(8,128)} %kappa_down.1, ...), custom_call_target="tpu_custom_call", output_to_operand_aliasing={{}: (8, {})} | custom-call | flops 10000000 | bytes 8388608 | tf_op jit(solution)/shard_map/ends/pallas_call | solution.py:326
Async XLA Ops:
  7.1 18.7 %collective-permute-start.1 = (f32[64,1,2048]{2,1,0:T(1,128)S(1)}, f32[64,1,2048]{2,1,0:T(1,128)S(1)}, u32[]{:S(2)}, u32[]{:S(2)}) collective-permute-start(f32[64,1,2048]{2,1,0:T(1,128)S(1)} %get-tuple-element.17), channel_id=1, source_target_pairs={{0,240},{16,0},{32,16},{48,32},{64,48},{80,64},{96,80},{112,96},{1... | collective-permute-start | bytes 1572872 | tf_op jit(solution)/shard_map/ppermute | solution.py:370
  14.6 17.0 %collective-permute-start = (f32[64,1,2048]{2,1,0:T(1,128)S(1)}, f32[64,1,2048]{2,1,0:T(1,128)S(1)}, u32[]{:S(2)}, u32[]{:S(2)}) collective-permute-start(f32[64,1,2048]{2,1,0:T(1,128)S(1)} %get-tuple-element.18), channel_id=1, source_target_pairs={{0,16},{16,32},{32,48},{48,64},{64,80},{80,96},{96,112},{112,128},... | collective-permute-start | bytes 1572872 | tf_op jit(solution)/shard_map/ppermute | solution.py:371
  25.8 6.6 %copy-start = (f32[64,1,2048]{2,1,0:T(1,128)}, f32[64,1,2048]{2,1,0:T(1,128)S(1)}, u32[]{:S(2)}) copy-start(f32[64,1,2048]{2,1,0:T(1,128)S(1)} %collective-permute-done.1.after) | copy-start | bytes 1572868
  31.6 0.8 copy-start.1
  35.0 41.8 %collective-permute-start.2 = (f32[7,8,2048]{2,1,0:T(8,128)}, f32[7,8,2048]{2,1,0:T(8,128)S(1)}, u32[]{:S(2)}, u32[]{:S(2)}) collective-permute-start(f32[7,8,2048]{2,1,0:T(8,128)} %get-tuple-element.11), channel_id=1, source_target_pairs={{0,1},{1,2},{2,3},{3,4},{4,5},{5,6},{6,7},{7,8},{8,9},{9,10},{10,1... | collective-permute-start | bytes 1376264 | tf_op jit(solution)/shard_map/ppermute | solution.py:381
  35.0 41.8 %collective-permute-start.3 = (f32[7,8,2048]{2,1,0:T(8,128)}, f32[7,8,2048]{2,1,0:T(8,128)S(1)}, u32[]{:S(2)}, u32[]{:S(2)}) collective-permute-start(f32[7,8,2048]{2,1,0:T(8,128)} %get-tuple-element.12), channel_id=1, source_target_pairs={{0,15},{1,0},{2,1},{3,2},{4,3},{5,4},{6,5},{7,6},{8,7},{9,8},{10,9... | collective-permute-start | bytes 1376264 | tf_op jit(solution)/shard_map/ppermute | solution.py:380
  76.8 0.8 copy-start.2
  76.8 0.9 %copy-start.3 = (f32[7,8,2048]{2,1,0:T(8,128)}, f32[7,8,2048]{2,1,0:T(8,128)S(1)}, u32[]{:S(2)}) copy-start(f32[7,8,2048]{2,1,0:T(8,128)S(1)} %collective-permute-done.3.from_down) | copy-start | bytes 1376260

commit v2 on v0

v2 whole, which is shorter than its diff:
```python
import jax
import jax.numpy as jnp
from jax import lax
from jax.experimental import pallas as pl
from jax.experimental.pallas import tpu as pltpu
from jax.sharding import PartitionSpec as P

STEPS = 6
NV = 16
LANES = 128
TILE = (8, LANES)
F32 = jnp.float32
GROUP = 4
BLOCK = 8
PAD = GROUP
FILL = 29 * 256
PARAMS = pltpu.CompilerParams(vmem_limit_bytes=62 * 2**20)
VMEM, HBM, SMEM = (pl.BlockSpec(memory_space=space) for space in (pltpu.VMEM, pltpu.HBM, pltpu.SMEM))


def cost(flops, mebibytes):
    return pl.CostEstimate(flops=flops, bytes_accessed=int(mebibytes * 2**20), transcendentals=0)


def iota(dim):
    return lax.broadcasted_iota(jnp.int32, TILE, dim)


def lanes(j):
    return pl.ds(LANES * j, LANES)


def tiles(*lead):
    return pltpu.VMEM((*lead, *TILE), F32)


def put_ghosts(rows, ghosts, start, count, batch=8):
    lane, slot = iota(1), iota(0)
    pending = []
    for first in range(0, count + batch, batch):
        made = []
        for k in range(first, min(first + batch, count)):
            west, east = pltpu.roll(rows[start + k, NV - 1], 1, 0), pltpu.roll(rows[start + k, 0], 7, 0)
            made.append((k, west, east, pltpu.roll(west, 8, 1), pltpu.roll(east, LANES - 8, 1)))
        for k, west, east, moved_west, moved_east in pending:
            ghosts[start + k, 0] = jnp.where(slot == 0, jnp.where(lane >= 8, moved_west, 0.0), west)
            ghosts[start + k, 1] = jnp.where(slot == 7, jnp.where(lane < LANES - 8, moved_east, 0.0), east)
        pending = made


def to_columns(natural, scratch):
    scratch[...] = jnp.concatenate(natural, axis=0).T


def from_columns(scratch, rows, row):
    for i in range(NV):
        rows[row, i] = scratch[pl.ds(i, 8, stride=NV), :]


def transpose_in(natural, rows, scratch, first, n_blocks, arrive):
    def iteration(b, stages):
        if 1 in stages:
            for q in range(BLOCK):
                from_columns(scratch.at[(b - 1) & 1, q], rows, first + (b - 1) * BLOCK + q)
        if 0 in stages:
            for q in range(BLOCK):
                to_columns(natural(b * BLOCK + q), scratch.at[b & 1, q])

    def body(b, carry):
        iteration(b, (0, 1))
        return carry

    done = 0
    for upto, ready in arrive:
        ready()
        if done == 0:
            iteration(0, (0,))
            done = 1
        lax.fori_loop(done, upto, body, 0)
        done = upto
    iteration(n_blocks, (1,))


def transpose_out(rows, scratch, starts, put):
    for b in range(len(starts) + 1):
        if b > 0:
            for q in range(BLOCK):
                flipped = scratch[(b - 1) & 1, q].T
                put(b - 1, q, [flipped[8 * j : 8 * j + 8] for j in range(NV)])
        if b < len(starts):
            for q in range(BLOCK):
                for i in range(NV):
                    scratch[b & 1, q, pl.ds(i, 8, stride=NV), :] = rows[starts[b] + q, i]


def face_row(half, half_ghosts, east, south, row, shift, with_south=True):
    here = [half_ghosts[row, 0], *[half[row, i] for i in range(NV)], half_ghosts[row, 1]]
    for i in range(NV + 1):
        east[row + shift, i] = here[i] + here[i + 1]
    if with_south:
        for i in range(NV):
            south[row + shift, i] = here[i + 1] + half[row + 1, i]


def diffuse(src, src_ghosts, dst, dst_ghosts, east, south, lo, count):
    def group(k, carry):
        base = lo + k * GROUP
        v, north = carry[:NV], carry[NV:]
        for q in range(GROUP):
            row = base + q
            below = [src[row + 1, i] for i in range(NV)]
            west = east[row, 0] * (v[0] - src_ghosts[row, 0])
            flux = []
            for i in range(NV):
                v_east = v[i + 1] if i + 1 < NV else src_ghosts[row, 1]
                here = east[row, i + 1] * (v_east - v[i])
                under = south[row, i] * (below[i] - v[i])
                dst[row, i] = (v[i] + (here - west)) + (under - north[i])
                west = here
                flux.append(under)
            v, north = below, flux
        return (*v, *north)

    v = [src[lo, i] for i in range(NV)]
    north = [south[lo - 1, i] * (v[i] - src[lo - 1, i]) for i in range(NV)]
    lax.fori_loop(0, count // GROUP, group, (*v, *north))
    put_ghosts(dst, dst_ghosts, lo, count)


def all_steps(one, two, east, south, first, rows, after_step=None):
    for step in range(1, STEPS + 1):
        src, dst = (one, two) if step % 2 else (two, one)
        count = -(-(rows - 2 * step) // GROUP) * GROUP
        diffuse(*src, *dst, east, south, first + step, count)
        if after_step is not None and step < STEPS:
            after_step(dst)


def own_coef(diag, lower, upper):
    slot, slots = iota(0), diag.shape[0]
    made = []
    for ref, shift in ((diag, 0), (lower, 1), (upper, -1)):
        value = jnp.zeros(TILE, F32)
        for t in range(slots):
            if 0 <= t + shift < slots:
                value = jnp.where(slot == t, ref[t + shift], value)
        made.append(value)
    return made


def edge_scales(lower, upper):
    tm, groups = lax.axis_index("tm"), lax.axis_size("tm")
    slots = lower.shape[0]
    return jnp.where(tm == groups - 1, 0.0, upper[slots - 1]), jnp.where(tm == 0, 0.0, lower[0])


class Copies:
    def __init__(self, sems):
        self.sems, self.used = sems, 0

    def start(self, src, dst):
        made = pltpu.make_async_copy(src, dst, self.sems.at[self.used])
        self.used += 1
        made.start()
        return made


def wait(copies):
    for made in copies:
        made.wait()


KAPPA, PACK = STEPS, STEPS + 1


def packs_kernel(field, kappa, go, pack_up, pack_down, field_v, kappa_v, sems):
    del go
    rows = field.shape[0]
    copies = Copies(sems)
    sides = ((pack_up, 0, 0), (pack_down, rows - STEPS, rows - 8))
    loads = [
        [copies.start(field.at[pl.ds(start, STEPS)], field_v.at[side]), copies.start(kappa.at[pl.ds(tile, 8)], kappa_v.at[side])]
        for side, (_, start, tile) in enumerate(sides)
    ]
    stores = []
    for side, (pack, _, _) in enumerate(sides):
        wait(loads[side])
        stores += [copies.start(field_v.at[side], pack.at[pl.ds(0, STEPS)]), copies.start(kappa_v.at[side], pack.at[KAPPA])]
    wait(stores)


def packs(fields, kappa, go):
    _, slots, width = fields.shape
    pack = jax.ShapeDtypeStruct((PACK, slots, width), F32)
    return pl.pallas_call(
        packs_kernel,
        out_shape=(pack, pack),
        in_specs=[HBM, HBM, HBM],
        out_specs=(HBM, HBM),
        scratch_shapes=[pltpu.VMEM((2, STEPS, slots, width), F32), pltpu.VMEM((2, 8, width), F32), pltpu.SemaphoreType.DMA((8,))],
        compiler_params=PARAMS,
        cost_estimate=cost(10**5, 2),
        name="packs",
    )(fields, kappa, go)


def pick_kernel(lower, upper, field, up, down, field_v, up_v, down_v, sems):
    rows = field.shape[0]
    copies = Copies(sems)
    cuts = [rows * k // 4 for k in range(5)]
    parts = [pl.ds(a, b - a) for a, b in zip(cuts[:-1], cuts[1:], strict=True)]
    loads = [copies.start(field.at[part], field_v.at[part]) for part in parts]
    up_scale, down_scale = edge_scales(lower, upper)
    stores = []

    def body(row, carry):
        up_v[row] = up_scale * field_v[row, 7:8, :]
        down_v[row] = down_scale * field_v[row, 0:1, :]
        return carry

    for part, load in zip(parts, loads, strict=True):
        load.wait()
        lax.fori_loop(part.start, part.start + part.size, body, 0, unroll=2)
        stores += [copies.start(up_v.at[part], up.at[part]), copies.start(down_v.at[part], down.at[part])]
    wait(stores)


def pick(lower, upper, fields):
    rows, slots, width = fields.shape
    edge = jax.ShapeDtypeStruct((rows, 1, width), F32)
    return pl.pallas_call(
        pick_kernel,
        out_shape=(edge, edge),
        in_specs=[SMEM, SMEM, HBM],
        out_specs=(HBM, HBM),
        scratch_shapes=[
            pltpu.VMEM(fields.shape, F32),
            pltpu.VMEM(edge.shape, F32),
            pltpu.VMEM(edge.shape, F32),
            pltpu.SemaphoreType.DMA((12,)),
        ],
        compiler_params=PARAMS,
        cost_estimate=cost(10**6, 5),
        name="pick",
    )(lower, upper, fields)


def faces_kernel(kappa, east_out, south_out, half, ghosts, east, south, scratch, sems):
    rows = kappa.shape[0]
    n_blocks = rows // BLOCK
    copies = Copies(sems)
    stores = []
    for i in range(NV):
        half[rows, i] = jnp.zeros(TILE, F32)
    for b in range(n_blocks + 1):
        if b >= 1:
            for q in range(BLOCK):
                from_columns(scratch.at[(b - 1) & 1, q], half, (b - 1) * BLOCK + q)
        if b < n_blocks:
            for q in range(BLOCK):
                row = b * BLOCK + q
                to_columns([jnp.broadcast_to(0.5 * kappa[row : row + 1, lanes(j)], TILE) for j in range(NV)], scratch.at[b & 1, q])
    put_ghosts(half, ghosts, 0, rows)
    for b in range(n_blocks):
        for q in range(BLOCK):
            face_row(half, ghosts, east, south, b * BLOCK + q, 0)
        at = pl.ds(b * BLOCK, BLOCK)
        stores += [copies.start(east.at[at], east_out.at[at]), copies.start(south.at[at], south_out.at[at])]
    wait(stores)


def faces(kappa):
    rows = kappa.shape[0]
    return pl.pallas_call(
        faces_kernel,
        out_shape=(jax.ShapeDtypeStruct((rows, NV + 1, *TILE), F32), jax.ShapeDtypeStruct((rows, NV, *TILE), F32)),
        in_specs=[VMEM],
        out_specs=(HBM, HBM),
        scratch_shapes=[
            tiles(rows + 1, NV),
            tiles(rows, 2),
            tiles(rows, NV + 1),
            tiles(rows, NV),
            pltpu.VMEM((2, BLOCK, LANES, LANES), F32),
            pltpu.SemaphoreType.DMA((2 * (rows // BLOCK),)),
        ],
        compiler_params=PARAMS,
        cost_estimate=cost(2 * 10**7, 9),
        name="faces",
    )(kappa)


def state(rows):
    return [tiles(rows, NV), tiles(rows, 2), tiles(rows, NV), tiles(rows, 2), tiles(rows, NV + 1), tiles(rows, NV)]


def mix(coef, x, before, after):
    slot = iota(0)
    later = jnp.where(slot == 7, jnp.broadcast_to(after, TILE), coef[1] * pltpu.roll(x, 7, 0))
    earlier = jnp.where(slot == 0, jnp.broadcast_to(before, TILE), coef[2] * pltpu.roll(x, 1, 0))
    return coef[0] * x + later + earlier


def corners_kernel(before, after, go, first, last, first_v, last_v, sems):
    del go
    rows = before.shape[0]
    copies = Copies(sems)
    loads, stores = [], []
    for held, start in ((first_v, 0), (last_v, rows - STEPS)):
        loads.append([copies.start(src.at[pl.ds(start, STEPS)], held.at[pl.ds(STEPS * k, STEPS)]) for k, src in enumerate((before, after))])
    for load, held, out in zip(loads, (first_v, last_v), (first, last), strict=True):
        wait(load)
        stores.append(copies.start(held, out))
    wait(stores)


def corners(before, after, go):
    edge = jax.ShapeDtypeStruct((2 * STEPS, *before.shape[1:]), F32)
    held = pltpu.VMEM(edge.shape, F32)
    return pl.pallas_call(
        corners_kernel,
        out_shape=(edge, edge),
        in_specs=[HBM, HBM, HBM],
        out_specs=(HBM, HBM),
        scratch_shapes=[held, held, pltpu.SemaphoreType.DMA((6,))],
        compiler_params=PARAMS,
        cost_estimate=cost(10**5, 1),
        name="corners",
    )(before, after, go)


def slab_kernel(diag, lower, upper, field, kappa, before, after, from_up, from_down, far_up, far_down, east_own, south_own, result, field_v, before_v, after_v, far_v, kappa_v, half, half_ghosts, one, one_g, two, two_g, east, south, scratch, sems, fill):
    total = field.shape[0]
    span = total + 2 * STEPS
    fill[0] = jnp.zeros(TILE, F32)
    fill[FILL - 1] = jnp.zeros(TILE, F32)
    copies = Copies(sems)
    kappa_in = []
    for at, (src, row) in enumerate(((from_up.at[KAPPA], None), (kappa, 0), (kappa, total - 8), (from_down.at[KAPPA], None))):
        kappa_in.append(copies.start(src if row is None else src.at[pl.ds(row, 8)], kappa_v.at[pl.ds(8 * at, 8)]))
    halo_in = [
        copies.start(from_up.at[pl.ds(0, STEPS)], field_v.at[pl.ds(total, STEPS)]),
        copies.start(from_down.at[pl.ds(0, STEPS)], field_v.at[pl.ds(total + STEPS, STEPS)]),
        copies.start(far_up, far_v.at[0]),
        copies.start(far_down, far_v.at[1]),
    ]
    quarter = total // 4
    field_in = []
    for k in range(4):
        at = pl.ds(k * quarter, quarter)
        field_in.append([copies.start(src.at[at], dst.at[at]) for src, dst in ((field, field_v), (before, before_v), (after, after_v))])
    faces_in = [
        copies.start(east_own, east.at[pl.ds(STEPS, total)]),
        copies.start(south_own.at[pl.ds(0, total - 1)], south.at[pl.ds(STEPS, total - 1)]),
    ]
    space, slabs = lax.axis_index("space"), lax.axis_size("space")
    at_top, at_bottom = space == 0, space == slabs - 1
    coef = own_coef(diag, lower, upper)

    wait(kappa_in)
    for edge, start in ((at_top, 0), (at_bottom, 24)):

        @pl.when(edge)
        def _(start=start):
            kappa_v[pl.ds(start, 8), :] = jnp.zeros((8, kappa_v.shape[1]), F32)

    sources = [*range(2, 9), *range(23, 30)]
    for k, row in enumerate(sources):
        spread = [jnp.broadcast_to(0.5 * kappa_v[row : row + 1, lanes(j)], TILE) for j in range(NV)]
        to_columns(spread, scratch.at[k // BLOCK, k % BLOCK])
    for k in range(len(sources)):
        from_columns(scratch.at[k // BLOCK, k % BLOCK], half, k)
    put_ghosts(half, half_ghosts, 0, len(sources))
    own_end = STEPS + total
    for k in range(STEPS):
        face_row(half, half_ghosts, east, south, k, 0)
        face_row(half, half_ghosts, east, south, STEPS + 2 + k, own_end - STEPS - 2, with_south=k < STEPS - 1)
    for i in range(NV):
        south[own_end - 1, i] = half[STEPS + 1, i] + half[STEPS + 2, i]

    wait(halo_in)
    for k in range(2 * STEPS):
        side, q = divmod(k, STEPS)
        near = [far_v[side, q], far_v[side, STEPS + q]]
        halo = [mix(coef, field_v[total + k, :, lanes(j)], *[x[:, LANES * j : LANES * (j + 1)] for x in near]) for j in range(NV)]
        to_columns(halo, scratch.at[k // BLOCK, k % BLOCK])
    for k in range(2 * STEPS):
        from_columns(scratch.at[k // BLOCK, k % BLOCK], one, k if k < STEPS else own_end + k - STEPS)

    def mixed(row):
        return [mix(coef, field_v[row, :, lanes(j)], before_v[row, :, lanes(j)], after_v[row, :, lanes(j)]) for j in range(NV)]

    arrive = [((k + 1) * quarter // BLOCK, lambda k=k: wait(field_in[k])) for k in range(4)]
    transpose_in(mixed, one, scratch, STEPS, total // BLOCK, arrive)
    put_ghosts(one, one_g, 0, span)

    def clear(state):
        rows, ghosts = state
        for edge, start in ((at_top, 0), (at_bottom, own_end)):

            @pl.when(edge)
            def _(start=start):
                for k in range(STEPS):
                    for i in range(NV):
                        rows[start + k, i] = jnp.zeros(TILE, F32)
                    ghosts[start + k, 0] = jnp.zeros(TILE, F32)
                    ghosts[start + k, 1] = jnp.zeros(TILE, F32)

    clear((one, one_g))
    wait(faces_in)
    all_steps((one, one_g), (two, two_g), east, south, 0, span, clear)
    stores = []

    def put(b, q, vregs):
        row = b * BLOCK + q
        for j, v in enumerate(vregs):
            field_v[row, :, lanes(j)] = v
        if q == BLOCK - 1:
            at = pl.ds(b * BLOCK, BLOCK)
            stores.append(copies.start(field_v.at[at], result.at[at]))

    transpose_out(one, scratch, list(range(STEPS, own_end, BLOCK)), put)
    wait(stores)


def slab(diag, lower, upper, fields, kappa, before, after, from_up, from_down, far_up, far_down, east, south):
    rows, slots, width = fields.shape
    span = rows + 2 * STEPS
    edge = pltpu.VMEM(before.shape, F32)
    return pl.pallas_call(
        slab_kernel,
        out_shape=jax.ShapeDtypeStruct(fields.shape, F32),
        in_specs=[SMEM, SMEM, SMEM, *[HBM] * 10],
        out_specs=HBM,
        scratch_shapes=[
            pltpu.VMEM((span, slots, width), F32),
            edge,
            edge,
            pltpu.VMEM((2, *far_up.shape), F32),
            pltpu.VMEM((32, width), F32),
            tiles(2 * STEPS + 3, NV),
            tiles(2 * STEPS + 2, 2),
            *state(span + 2 * PAD),
            pltpu.VMEM((2, BLOCK, LANES, LANES), F32),
            pltpu.SemaphoreType.DMA((32,)),
            tiles(FILL),
        ],
        compiler_params=PARAMS,
        cost_estimate=cost(4 * 10**8, 16),
        name="slab",
    )(diag, lower, upper, fields, kappa, before, after, from_up, from_down, far_up, far_down, east, south)


def ring(axis, step):
    size = lax.axis_size(axis)
    return [(i, (i + step) % size) for i in range(size)]


def local(forcing, kappa, diag, lower, upper):
    up, down = pick(lower, upper, forcing)
    before = lax.ppermute(up, "tm", ring("tm", 1))
    after = lax.ppermute(down, "tm", ring("tm", -1))
    pack_up, pack_down = packs(forcing, kappa, down)
    from_down = lax.ppermute(pack_up, "space", ring("space", -1))
    from_up = lax.ppermute(pack_down, "space", ring("space", 1))
    east, south = faces(kappa)
    first, last = corners(before, after, east)
    far_down = lax.ppermute(first, "space", ring("space", -1))
    far_up = lax.ppermute(last, "space", ring("space", 1))
    return slab(diag, lower, upper, forcing, kappa, before, after, from_up, from_down, far_up, far_down, east, south)


def solution(mesh):
    return jax.shard_map(
        local,
        mesh=mesh,
        in_specs=(P("space", "tm", None), P("space", None), P("tm"), P("tm"), P("tm")),
        out_specs=P("space", "tm", None),
        check_vma=False,
    )
```

time: 237 us -> 53.6 us (0.23)
  the two profiles are of different devices: /device:TPU:29 before, /device:TPU:27 now
where the time goes in v2:
time: 53.6 us; the launch traced here: 53.4 us
  Pallas kernels  32.2 us (60%)
  starting transfers between devices  11.5 us (21%)
  waiting for transfers between devices  7.84 us (15%)
  local copies, waits for them, and re-layouts  1.66 us (3%)
    pallas_call x1, Pallas kernels, slab(): pl.pallas_call(slab_kernel, out_shape=jax.ShapeDtypeStruct(fields.shape,...  18.3 us
    pallas_call x1, Pallas kernels, faces(): pl.pallas_call(faces_kernel, out_shape=(jax.ShapeDtypeStruct((rows, NV +...  6.53 us
    ppermute x1, starting transfers between devices, local(): after = lax.ppermute(down, 'tm', ring('tm', -1))  5.59 us
    ppermute x1, waiting for transfers between devices, local(): far_down = lax.ppermute(first, 'space', ring('space', -1))  4.4 us
    pallas_call x1, Pallas kernels, pick(): pl.pallas_call(pick_kernel, out_shape=(edge, edge), in_specs=[SMEM, SMEM,...  3.72 us
    ppermute x1, starting transfers between devices, local(): far_up = lax.ppermute(last, 'space', ring('space', 1))  2.44 us
    pallas_call x1, Pallas kernels, packs(): pl.pallas_call(packs_kernel, out_shape=(pack, pack), in_specs=[HBM, HBM,...  2.03 us
    ppermute x1, waiting for transfers between devices, local(): far_up = lax.ppermute(last, 'space', ring('space', 1))  1.92 us
  transfers between devices with their start and end apart: 6, of which 3 were waited for; matrix products, arithmetic and copies ran while one was open for 0% of the time, Pallas kernels for 19%

profile of v2, /device:TPU:27, one launch (start us, length us, event | category | flops | bytes accessed | tf_op | source)
XLA Modules:
  0.0 53.4 jit_solution(12620112016432643106)
XLA Ops:
  0.0 3.7 %pick.1 = (f32[64,1,2048]{2,1,0:T(1,128)}, f32[64,1,2048]{2,1,0:T(1,128)}) custom-call(f32[8]{0:T(128)} %lower.3, f32[8]{0:T(128)} %upper.3, f32[64,8,2048]{2,1,0:T(8,128)} %field.5), custom_call_target="tpu_custom_call" | custom-call | flops 1000000 | bytes 5242880 | tf_op jit(solution)/shard_map/pick/pallas_call | solution.py:231
  3.7 1.7 %collective-permute-start = (f32[64,1,2048]{2,1,0:T(1,128)}, f32[64,1,2048]{2,1,0:T(1,128)S(1)}, u32[]{:S(2)}, u32[]{:S(2)}) collective-permute-start(f32[64,1,2048]{2,1,0:T(1,128)} %get-tuple-element.13), channel_id=1, source_target_pairs={{0,16},{16,32},{32,48},{48,64},{64,80},{80,96},{96,112},{112,128},... | collective-permute-start | bytes 1572872 | tf_op jit(solution)/shard_map/ppermute | solution.py:461
  5.4 5.6 %collective-permute-start.1 = (f32[64,1,2048]{2,1,0:T(1,128)}, f32[64,1,2048]{2,1,0:T(1,128)S(1)}, u32[]{:S(2)}, u32[]{:S(2)}) collective-permute-start(f32[64,1,2048]{2,1,0:T(1,128)} %get-tuple-element.14.go), channel_id=1, source_target_pairs={{0,240},{16,0},{32,16},{48,32},{64,48},{80,64},{96,80},{112,96},{1... | collective-permute-start | bytes 1572872 | tf_op jit(solution)/shard_map/ppermute | solution.py:462
  11.0 2.0 %packs.1 = (f32[7,8,2048]{2,1,0:T(8,128)}, f32[7,8,2048]{2,1,0:T(8,128)}) custom-call(f32[64,8,2048]{2,1,0:T(8,128)} %field.5, f32[64,2048]{1,0:T(8,128)} %kappa.5, f32[64,1,2048]{2,1,0:T(1,128)} %get-tuple-element.14.go), custom_call_target="tpu_custom_call" | custom-call | flops 100000 | bytes 2097152 | tf_op jit(solution)/shard_map/packs/pallas_call | solution.py:195
  13.1 1.7 %collective-permute-start.2 = (f32[7,8,2048]{2,1,0:T(8,128)}, f32[7,8,2048]{2,1,0:T(8,128)S(1)}, u32[]{:S(2)}, u32[]{:S(2)}) collective-permute-start(f32[7,8,2048]{2,1,0:T(8,128)} %get-tuple-element.15), channel_id=1, source_target_pairs={{0,1},{1,2},{2,3},{3,4},{4,5},{5,6},{6,7},{7,8},{8,9},{9,10},{10,1... | collective-permute-start | bytes 1376264 | tf_op jit(solution)/shard_map/ppermute | solution.py:465
  14.8 0.0 collective-permute-start.3
  14.8 6.5 %faces.1 = (f32[64,17,8,128]{3,2,1,0:T(8,128)}, f32[64,16,8,128]{3,2,1,0:T(8,128)}) custom-call(f32[64,2048]{1,0:T(8,128)} %kappa.5), custom_call_target="tpu_custom_call" | custom-call | flops 20000000 | bytes 9437184 | tf_op jit(solution)/shard_map/faces/pallas_call | solution.py:274
  21.3 1.5 %collective-permute-done.before = f32[64,1,2048]{2,1,0:T(1,128)S(1)} collective-permute-done((f32[64,1,2048]{2,1,0:T(1,128)}, f32[64,1,2048]{2,1,0:T(1,128)S(1)}, u32[]{:S(2)}, u32[]{:S(2)}) %collective-permute-start) | collective-permute-done | bytes 524320 | tf_op jit(solution)/shard_map/ppermute | solution.py:461
  22.8 0.0 copy-start
  22.8 0.0 collective-permute-done.1.after
  22.8 0.0 copy-start.1
  22.8 0.9 %copy-done = f32[64,1,2048]{2,1,0:T(1,128)} copy-done((f32[64,1,2048]{2,1,0:T(1,128)}, f32[64,1,2048]{2,1,0:T(1,128)S(1)}, u32[]{:S(2)}) %copy-start) | copy-done | bytes 524312
  23.7 0.2 copy-done.1
  23.9 1.6 %corners.1 = (f32[12,1,2048]{2,1,0:T(1,128)}, f32[12,1,2048]{2,1,0:T(1,128)}) custom-call(f32[64,1,2048]{2,1,0:T(1,128)} %copy-done, f32[64,1,2048]{2,1,0:T(1,128)} %copy-done.1, f32[64,17,8,128]{3,2,1,0:T(8,128)} %get-tuple-element.17.go.east_own), custom_call_target="tpu_custom_call" | custom-call | flops 100000 | bytes 1048576 | tf_op jit(solution)/shard_map/corners/pallas_call | solution.py:320
  25.4 2.4 %collective-permute-start.4 = (f32[12,1,2048]{2,1,0:T(1,128)}, f32[12,1,2048]{2,1,0:T(1,128)S(1)}, u32[]{:S(2)}, u32[]{:S(2)}) collective-permute-start(f32[12,1,2048]{2,1,0:T(1,128)} %get-tuple-element.18), channel_id=1, source_target_pairs={{0,1},{1,2},{2,3},{3,4},{4,5},{5,6},{6,7},{7,8},{8,9},{9,10},{10,1... | collective-permute-start | bytes 294920 | tf_op jit(solution)/shard_map/ppermute | solution.py:469
  27.9 0.0 collective-permute-start.5
  27.9 0.0 collective-permute-done.2.from_up
  27.9 0.0 copy-start.2
  27.9 0.0 collective-permute-done.3.from_down
  27.9 0.0 copy-start.3
  27.9 1.9 %collective-permute-done.4.far_up = f32[12,1,2048]{2,1,0:T(1,128)S(1)} collective-permute-done((f32[12,1,2048]{2,1,0:T(1,128)}, f32[12,1,2048]{2,1,0:T(1,128)S(1)}, u32[]{:S(2)}, u32[]{:S(2)}) %collective-permute-start.4) | collective-permute-done | bytes 98336 | tf_op jit(solution)/shard_map/ppermute | solution.py:469
  29.8 0.0 copy-start.4
  29.8 4.4 %collective-permute-done.5.far_down = f32[12,1,2048]{2,1,0:T(1,128)S(1)} collective-permute-done((f32[12,1,2048]{2,1,0:T(1,128)}, f32[12,1,2048]{2,1,0:T(1,128)S(1)}, u32[]{:S(2)}, u32[]{:S(2)}) %collective-permute-start.5) | collective-permute-done | bytes 98336 | tf_op jit(solution)/shard_map/ppermute | solution.py:468
  34.2 0.0 copy-start.5
  34.2 0.0 copy-done.2
  34.2 0.0 copy-done.3
  34.2 0.0 copy-done.4
  34.3 0.6 %copy-done.5 = f32[12,1,2048]{2,1,0:T(1,128)} copy-done((f32[12,1,2048]{2,1,0:T(1,128)}, f32[12,1,2048]{2,1,0:T(1,128)S(1)}, u32[]{:S(2)}) %copy-start.5) | copy-done | bytes 98328
  34.9 18.3 %slab.1 = f32[64,8,2048]{2,1,0:T(8,128)} custom-call(f32[8]{0:T(128)} %diag.1, f32[8]{0:T(128)} %lower.3, f32[8]{0:T(128)} %upper.3, f32[64,8,2048]{2,1,0:T(8,128)} %field.5, f32[64,2048]{1,0:T(8,128)} %kappa.5, f32[64,1,2048]{2,1,0:T(1,128)} %copy-done, f32[64,1,2048]{2,1,0:T(1,128)} %copy-done.1, f32[7,8,2048]{2,1,0:T(8,128)} %copy-done.2, ...), custom_call_target="tpu_custom_call" | custom-call | flops 400000000 | bytes 16777216 | tf_op jit(solution)/shard_map/slab/pallas_call | solution.py:430
Async XLA Ops:
  3.7 19.1 %collective-permute-start = (f32[64,1,2048]{2,1,0:T(1,128)}, f32[64,1,2048]{2,1,0:T(1,128)S(1)}, u32[]{:S(2)}, u32[]{:S(2)}) collective-permute-start(f32[64,1,2048]{2,1,0:T(1,128)} %get-tuple-element.13), channel_id=1, source_target_pairs={{0,16},{16,32},{32,48},{48,64},{64,80},{80,96},{96,112},{112,128},... | collective-permute-start | bytes 1572872 | tf_op jit(solution)/shard_map/ppermute | solution.py:461
  5.4 17.4 %collective-permute-start.1 = (f32[64,1,2048]{2,1,0:T(1,128)}, f32[64,1,2048]{2,1,0:T(1,128)S(1)}, u32[]{:S(2)}, u32[]{:S(2)}) collective-permute-start(f32[64,1,2048]{2,1,0:T(1,128)} %get-tuple-element.14.go), channel_id=1, source_target_pairs={{0,240},{16,0},{32,16},{48,32},{64,48},{80,64},{96,80},{112,96},{1... | collective-permute-start | bytes 1572872 | tf_op jit(solution)/shard_map/ppermute | solution.py:462
  13.1 14.8 %collective-permute-start.2 = (f32[7,8,2048]{2,1,0:T(8,128)}, f32[7,8,2048]{2,1,0:T(8,128)S(1)}, u32[]{:S(2)}, u32[]{:S(2)}) collective-permute-start(f32[7,8,2048]{2,1,0:T(8,128)} %get-tuple-element.15), channel_id=1, source_target_pairs={{0,1},{1,2},{2,3},{3,4},{4,5},{5,6},{6,7},{7,8},{8,9},{9,10},{10,1... | collective-permute-start | bytes 1376264 | tf_op jit(solution)/shard_map/ppermute | solution.py:465
  14.8 13.1 %collective-permute-start.3 = (f32[7,8,2048]{2,1,0:T(8,128)}, f32[7,8,2048]{2,1,0:T(8,128)S(1)}, u32[]{:S(2)}, u32[]{:S(2)}) collective-permute-start(f32[7,8,2048]{2,1,0:T(8,128)} %get-tuple-element.16), channel_id=1, source_target_pairs={{0,15},{1,0},{2,1},{3,2},{4,3},{5,4},{6,5},{7,6},{8,7},{9,8},{10,9... | collective-permute-start | bytes 1376264 | tf_op jit(solution)/shard_map/ppermute | solution.py:464
  22.8 0.9 %copy-start = (f32[64,1,2048]{2,1,0:T(1,128)}, f32[64,1,2048]{2,1,0:T(1,128)S(1)}, u32[]{:S(2)}) copy-start(f32[64,1,2048]{2,1,0:T(1,128)S(1)} %collective-permute-done.before) | copy-start | bytes 1572868
  22.8 1.0 %copy-start.1 = (f32[64,1,2048]{2,1,0:T(1,128)}, f32[64,1,2048]{2,1,0:T(1,128)S(1)}, u32[]{:S(2)}) copy-start(f32[64,1,2048]{2,1,0:T(1,128)S(1)} %collective-permute-done.1.after) | copy-start | bytes 1572868
  25.4 4.4 %collective-permute-start.4 = (f32[12,1,2048]{2,1,0:T(1,128)}, f32[12,1,2048]{2,1,0:T(1,128)S(1)}, u32[]{:S(2)}, u32[]{:S(2)}) collective-permute-start(f32[12,1,2048]{2,1,0:T(1,128)} %get-tuple-element.18), channel_id=1, source_target_pairs={{0,1},{1,2},{2,3},{3,4},{4,5},{5,6},{6,7},{7,8},{8,9},{9,10},{10,1... | collective-permute-start | bytes 294920 | tf_op jit(solution)/shard_map/ppermute | solution.py:469
  27.9 6.4 %collective-permute-start.5 = (f32[12,1,2048]{2,1,0:T(1,128)}, f32[12,1,2048]{2,1,0:T(1,128)S(1)}, u32[]{:S(2)}, u32[]{:S(2)}) collective-permute-start(f32[12,1,2048]{2,1,0:T(1,128)} %get-tuple-element.19), channel_id=1, source_target_pairs={{0,15},{1,0},{2,1},{3,2},{4,3},{5,4},{6,5},{7,6},{8,7},{9,8},{10,9... | collective-permute-start | bytes 294920 | tf_op jit(solution)/shard_map/ppermute | solution.py:468
  27.9 6.4 %copy-start.2 = (f32[7,8,2048]{2,1,0:T(8,128)}, f32[7,8,2048]{2,1,0:T(8,128)S(1)}, u32[]{:S(2)}) copy-start(f32[7,8,2048]{2,1,0:T(8,128)S(1)} %collective-permute-done.2.from_up) | copy-start | bytes 1376260
  27.9 6.3 %copy-start.3 = (f32[7,8,2048]{2,1,0:T(8,128)}, f32[7,8,2048]{2,1,0:T(8,128)S(1)}, u32[]{:S(2)}) copy-start(f32[7,8,2048]{2,1,0:T(8,128)S(1)} %collective-permute-done.3.from_down) | copy-start | bytes 1376260
  29.8 4.4 %copy-start.4 = (f32[12,1,2048]{2,1,0:T(1,128)}, f32[12,1,2048]{2,1,0:T(1,128)S(1)}, u32[]{:S(2)}) copy-start(f32[12,1,2048]{2,1,0:T(1,128)S(1)} %collective-permute-done.4.far_up) | copy-start | bytes 294916
  34.2 0.6 %copy-start.5 = (f32[12,1,2048]{2,1,0:T(1,128)}, f32[12,1,2048]{2,1,0:T(1,128)S(1)}, u32[]{:S(2)}) copy-start(f32[12,1,2048]{2,1,0:T(1,128)S(1)} %collective-permute-done.5.far_down) | copy-start | bytes 294916

commit v3 on v2

--- a/solution.py
+++ b/solution.py
@@ -13,8 +13,9 @@
 GROUP = 4
 BLOCK = 8
 PAD = GROUP
-FILL = 29 * 256
-PARAMS = pltpu.CompilerParams(vmem_limit_bytes=62 * 2**20)
+FILL = 32 * 256
+MORE = 62 * 256
+PARAMS = pltpu.CompilerParams(vmem_limit_bytes=63 * 2**20 + 2**19)
 VMEM, HBM, SMEM = (pl.BlockSpec(memory_space=space) for space in (pltpu.VMEM, pltpu.HBM, pltpu.SMEM))
 
 
@@ -301,8 +302,10 @@
     return coef[0] * x + later + earlier
 
 
-def corners_kernel(before, after, go, first, last, first_v, last_v, sems):
+def corners_kernel(before, after, go, first, last, first_v, last_v, sems, fill):
     del go
+    fill[0] = jnp.zeros(TILE, F32)
+    fill[MORE - 1] = jnp.zeros(TILE, F32)
     rows = before.shape[0]
     copies = Copies(sems)
     loads, stores = [], []
@@ -322,7 +325,7 @@
         out_shape=(edge, edge),
         in_specs=[HBM, HBM, HBM],
         out_specs=(HBM, HBM),
-        scratch_shapes=[held, held, pltpu.SemaphoreType.DMA((6,))],
+        scratch_shapes=[held, held, pltpu.SemaphoreType.DMA((6,)), tiles(MORE)],
         compiler_params=PARAMS,
         cost_estimate=cost(10**5, 1),
         name="corners",

time: 53.6 us -> 52.2 us (0.974)
  local copies, waits for them, and re-layouts: 1.66 us -> 0.01 us
    unnamed x12 -> x2, local copies, waits for them, and re-layouts: 1.66 us -> 0.01 us
  transfers between devices with their start and end apart: 6 -> 6, of which waited for: 3 -> 3; matrix products, arithmetic and copies ran while one was open for 0% -> 0% of each run, Pallas kernels for 19% -> 20%
where the time goes in v3:
time: 52.2 us; the launch traced here: 52 us
  Pallas kernels  32.3 us (62%)
  starting transfers between devices  11.5 us (22%)
  waiting for transfers between devices  7.94 us (15%)
    pallas_call x1, Pallas kernels, slab(): pl.pallas_call(slab_kernel, out_shape=jax.ShapeDtypeStruct(fields.shape,...  18.4 us
    pallas_call x1, Pallas kernels, faces(): pl.pallas_call(faces_kernel, out_shape=(jax.ShapeDtypeStruct((rows, NV +...  6.67 us
    ppermute x1, starting transfers between devices, local(): after = lax.ppermute(down, 'tm', ring('tm', -1))  5.59 us
    ppermute x1, waiting for transfers between devices, local(): far_down = lax.ppermute(first, 'space', ring('space', -1))  4.51 us
    pallas_call x1, Pallas kernels, pick(): pl.pallas_call(pick_kernel, out_shape=(edge, edge), in_specs=[SMEM, SMEM,...  3.72 us
    ppermute x1, starting transfers between devices, local(): far_up = lax.ppermute(last, 'space', ring('space', 1))  2.46 us
    pallas_call x1, Pallas kernels, packs(): pl.pallas_call(packs_kernel, out_shape=(pack, pack), in_specs=[HBM, HBM,...  2 us
    ppermute x1, waiting for transfers between devices, local(): far_up = lax.ppermute(last, 'space', ring('space', 1))  1.93 us
  transfers between devices with their start and end apart: 6, of which 3 were waited for; matrix products, arithmetic and copies ran while one was open for 0% of the time, Pallas kernels for 20%

profile of v3, /device:TPU:27, one launch (start us, length us, event | category | flops | bytes accessed | tf_op | source)
XLA Modules:
  0.0 52.0 jit_solution(296228423783879472)
XLA Ops:
  0.0 3.7 %pick.1 = (f32[64,1,2048]{2,1,0:T(1,128)}, f32[64,1,2048]{2,1,0:T(1,128)}) custom-call(f32[8]{0:T(128)} %lower.3, f32[8]{0:T(128)} %upper.3, f32[64,8,2048]{2,1,0:T(8,128)} %field.5), custom_call_target="tpu_custom_call" | custom-call | flops 1000000 | bytes 5242880 | tf_op jit(solution)/shard_map/pick/pallas_call | solution.py:232
  3.7 1.7 %collective-permute-start = (f32[64,1,2048]{2,1,0:T(1,128)}, f32[64,1,2048]{2,1,0:T(1,128)}, u32[]{:S(2)}, u32[]{:S(2)}) collective-permute-start(f32[64,1,2048]{2,1,0:T(1,128)} %get-tuple-element.13), channel_id=1, source_target_pairs={{0,16},{16,32},{32,48},{48,64},{64,80},{80,96},{96,112},{112,128},... | collective-permute-start | bytes 1572872 | tf_op jit(solution)/shard_map/ppermute | solution.py:464
  5.4 5.6 %collective-permute-start.1 = (f32[64,1,2048]{2,1,0:T(1,128)}, f32[64,1,2048]{2,1,0:T(1,128)}, u32[]{:S(2)}, u32[]{:S(2)}) collective-permute-start(f32[64,1,2048]{2,1,0:T(1,128)} %get-tuple-element.14.go), channel_id=1, source_target_pairs={{0,240},{16,0},{32,16},{48,32},{64,48},{80,64},{96,80},{112,96},{1... | collective-permute-start | bytes 1572872 | tf_op jit(solution)/shard_map/ppermute | solution.py:465
  11.0 2.0 %packs.1 = (f32[7,8,2048]{2,1,0:T(8,128)}, f32[7,8,2048]{2,1,0:T(8,128)}) custom-call(f32[64,8,2048]{2,1,0:T(8,128)} %field.5, f32[64,2048]{1,0:T(8,128)} %kappa.5, f32[64,1,2048]{2,1,0:T(1,128)} %get-tuple-element.14.go), custom_call_target="tpu_custom_call" | custom-call | flops 100000 | bytes 2097152 | tf_op jit(solution)/shard_map/packs/pallas_call | solution.py:196
  13.1 1.7 %collective-permute-start.2 = (f32[7,8,2048]{2,1,0:T(8,128)}, f32[7,8,2048]{2,1,0:T(8,128)S(1)}, u32[]{:S(2)}, u32[]{:S(2)}) collective-permute-start(f32[7,8,2048]{2,1,0:T(8,128)} %get-tuple-element.15), channel_id=1, source_target_pairs={{0,1},{1,2},{2,3},{3,4},{4,5},{5,6},{6,7},{7,8},{8,9},{9,10},{10,1... | collective-permute-start | bytes 1376264 | tf_op jit(solution)/shard_map/ppermute | solution.py:468
  14.8 0.0 collective-permute-start.3
  14.8 6.7 %faces.1 = (f32[64,17,8,128]{3,2,1,0:T(8,128)}, f32[64,16,8,128]{3,2,1,0:T(8,128)}) custom-call(f32[64,2048]{1,0:T(8,128)} %kappa.5), custom_call_target="tpu_custom_call" | custom-call | flops 20000000 | bytes 9437184 | tf_op jit(solution)/shard_map/faces/pallas_call | solution.py:275
  21.5 1.5 %collective-permute-done.before = f32[64,1,2048]{2,1,0:T(1,128)} collective-permute-done((f32[64,1,2048]{2,1,0:T(1,128)}, f32[64,1,2048]{2,1,0:T(1,128)}, u32[]{:S(2)}, u32[]{:S(2)}) %collective-permute-start) | collective-permute-done | bytes 524320 | tf_op jit(solution)/shard_map/ppermute | solution.py:464
  23.0 0.0 collective-permute-done.1.after
  23.0 1.6 %corners.1 = (f32[12,1,2048]{2,1,0:T(1,128)}, f32[12,1,2048]{2,1,0:T(1,128)}) custom-call(f32[64,1,2048]{2,1,0:T(1,128)} %collective-permute-done.before, f32[64,1,2048]{2,1,0:T(1,128)} %collective-permute-done.1.after, f32[64,17,8,128]{3,2,1,0:T(8,128)} %get-tuple-element.17.go.east_own), custom_call_target="tpu_custom_call" | custom-call | flops 100000 | bytes 1048576 | tf_op jit(solution)/shard_map/corners/pallas_call | solution.py:323
  24.5 2.5 %collective-permute-start.4 = (f32[12,1,2048]{2,1,0:T(1,128)}, f32[12,1,2048]{2,1,0:T(1,128)}, u32[]{:S(2)}, u32[]{:S(2)}) collective-permute-start(f32[12,1,2048]{2,1,0:T(1,128)} %get-tuple-element.18), channel_id=1, source_target_pairs={{0,1},{1,2},{2,3},{3,4},{4,5},{5,6},{6,7},{7,8},{8,9},{9,10},{10,1... | collective-permute-start | bytes 294920 | tf_op jit(solution)/shard_map/ppermute | solution.py:472
  27.0 0.0 collective-permute-start.5
  27.0 0.0 collective-permute-done.2.from_up
  27.0 0.0 copy-start
  27.0 0.0 collective-permute-done.3.from_down
  27.0 1.9 %collective-permute-done.4.far_up = f32[12,1,2048]{2,1,0:T(1,128)} collective-permute-done((f32[12,1,2048]{2,1,0:T(1,128)}, f32[12,1,2048]{2,1,0:T(1,128)}, u32[]{:S(2)}, u32[]{:S(2)}) %collective-permute-start.4) | collective-permute-done | bytes 98336 | tf_op jit(solution)/shard_map/ppermute | solution.py:472
  28.9 4.5 %collective-permute-done.5.far_down = f32[12,1,2048]{2,1,0:T(1,128)} collective-permute-done((f32[12,1,2048]{2,1,0:T(1,128)}, f32[12,1,2048]{2,1,0:T(1,128)}, u32[]{:S(2)}, u32[]{:S(2)}) %collective-permute-start.5) | collective-permute-done | bytes 98336 | tf_op jit(solution)/shard_map/ppermute | solution.py:471
  33.4 0.0 copy-done
  33.4 18.4 %slab.1 = f32[64,8,2048]{2,1,0:T(8,128)} custom-call(f32[8]{0:T(128)} %diag.1, f32[8]{0:T(128)} %lower.3, f32[8]{0:T(128)} %upper.3, f32[64,8,2048]{2,1,0:T(8,128)} %field.5, f32[64,2048]{1,0:T(8,128)} %kappa.5, f32[64,1,2048]{2,1,0:T(1,128)} %collective-permute-done.before, f32[64,1,2048]{2,1,0:T(1,128)} %collective-permute-done.1.after, ...), custom_call_target="tpu_custom_call" | custom-call | flops 400000000 | bytes 16777216 | tf_op jit(solution)/shard_map/slab/pallas_call | solution.py:433
Async XLA Ops:
  3.7 19.2 %collective-permute-start = (f32[64,1,2048]{2,1,0:T(1,128)}, f32[64,1,2048]{2,1,0:T(1,128)}, u32[]{:S(2)}, u32[]{:S(2)}) collective-permute-start(f32[64,1,2048]{2,1,0:T(1,128)} %get-tuple-element.13), channel_id=1, source_target_pairs={{0,16},{16,32},{32,48},{48,64},{64,80},{80,96},{96,112},{112,128},... | collective-permute-start | bytes 1572872 | tf_op jit(solution)/shard_map/ppermute | solution.py:464
  5.4 17.5 %collective-permute-start.1 = (f32[64,1,2048]{2,1,0:T(1,128)}, f32[64,1,2048]{2,1,0:T(1,128)}, u32[]{:S(2)}, u32[]{:S(2)}) collective-permute-start(f32[64,1,2048]{2,1,0:T(1,128)} %get-tuple-element.14.go), channel_id=1, source_target_pairs={{0,240},{16,0},{32,16},{48,32},{64,48},{80,64},{96,80},{112,96},{1... | collective-permute-start | bytes 1572872 | tf_op jit(solution)/shard_map/ppermute | solution.py:465
  13.1 13.9 %collective-permute-start.2 = (f32[7,8,2048]{2,1,0:T(8,128)}, f32[7,8,2048]{2,1,0:T(8,128)S(1)}, u32[]{:S(2)}, u32[]{:S(2)}) collective-permute-start(f32[7,8,2048]{2,1,0:T(8,128)} %get-tuple-element.15), channel_id=1, source_target_pairs={{0,1},{1,2},{2,3},{3,4},{4,5},{5,6},{6,7},{7,8},{8,9},{9,10},{10,1... | collective-permute-start | bytes 1376264 | tf_op jit(solution)/shard_map/ppermute | solution.py:468
  14.8 12.2 %collective-permute-start.3 = (f32[7,8,2048]{2,1,0:T(8,128)}, f32[7,8,2048]{2,1,0:T(8,128)}, u32[]{:S(2)}, u32[]{:S(2)}) collective-permute-start(f32[7,8,2048]{2,1,0:T(8,128)} %get-tuple-element.16), channel_id=1, source_target_pairs={{0,15},{1,0},{2,1},{3,2},{4,3},{5,4},{6,5},{7,6},{8,7},{9,8},{10,9... | collective-permute-start | bytes 1376264 | tf_op jit(solution)/shard_map/ppermute | solution.py:467
  24.5 4.4 %collective-permute-start.4 = (f32[12,1,2048]{2,1,0:T(1,128)}, f32[12,1,2048]{2,1,0:T(1,128)}, u32[]{:S(2)}, u32[]{:S(2)}) collective-permute-start(f32[12,1,2048]{2,1,0:T(1,128)} %get-tuple-element.18), channel_id=1, source_target_pairs={{0,1},{1,2},{2,3},{3,4},{4,5},{5,6},{6,7},{7,8},{8,9},{9,10},{10,1... | collective-permute-start | bytes 294920 | tf_op jit(solution)/shard_map/ppermute | solution.py:472
  27.0 6.5 %collective-permute-start.5 = (f32[12,1,2048]{2,1,0:T(1,128)}, f32[12,1,2048]{2,1,0:T(1,128)}, u32[]{:S(2)}, u32[]{:S(2)}) collective-permute-start(f32[12,1,2048]{2,1,0:T(1,128)} %get-tuple-element.19), channel_id=1, source_target_pairs={{0,15},{1,0},{2,1},{3,2},{4,3},{5,4},{6,5},{7,6},{8,7},{9,8},{10,9... | collective-permute-start | bytes 294920 | tf_op jit(solution)/shard_map/ppermute | solution.py:471
  27.0 6.5 %copy-start = (f32[7,8,2048]{2,1,0:T(8,128)}, f32[7,8,2048]{2,1,0:T(8,128)S(1)}, u32[]{:S(2)}) copy-start(f32[7,8,2048]{2,1,0:T(8,128)S(1)} %collective-permute-done.2.from_up) | copy-start | bytes 1376260
